TPU v7x, 32 devices: a whole 2x2x4 slice. The times are simulated.
32 devices in a mesh: fsdp: 16 (over z, y, x), dp: 2 (over core).
Axes of the slice: x: 2, y: 2, z: 4, core: 2. Of those that a mesh axis runs over, the one named last changes fastest.
Arguments:
- tokens: bfloat16 [65536, 512], P(('fsdp', 'dp')), may hold values from -6 to 6
- cotangent: bfloat16 [65536, 512], P(('fsdp', 'dp')), may hold values from -6 to 6
- segment_ids: int32 [64, 1024], P(('fsdp', 'dp')), may hold values from 0 to 5, as said below
- valid_counts: int32 [64], P(('fsdp', 'dp')), may hold values from 768 to 960, as said below
- weight_qkv: float32 [512, 1536], P('fsdp'), may hold values from -0.25 to 0.25
- weight_out: float32 [512, 512], P('fsdp'), may hold values from -1 to 1
- weight_up: float32 [512, 2048], P('fsdp'), may hold values from -0.25 to 0.25
- weight_down: float32 [2048, 512], P('fsdp'), may hold values from -0.125 to 0.125
- vectors: float32 [8, 512], P(None, 'fsdp'), may hold values from -1.2 to 2.6, as said below
- up_bias: float32 [2048], P('fsdp'), may hold values from -1.5 to 1.5
- momentum_qkv: float32 [512, 1536], P('fsdp'), may hold values from -8 to 8
- momentum_out: float32 [512, 512], P('fsdp'), may hold values from -8 to 8
- momentum_up: float32 [512, 2048], P('fsdp'), may hold values from -8 to 8
- momentum_down: float32 [2048, 512], P('fsdp'), may hold values from -8 to 8
- momentum_vectors: float32 [8, 512], P(None, 'fsdp'), may hold values from -32 to 32
- momentum_bias: float32 [2048], P('fsdp'), may hold values from -4 to 4
- squares_qkv: float32 [512, 1536], P('fsdp'), may hold values from 1.6384 to 6.5536
- squares_out: float32 [512, 512], P('fsdp'), may hold values from 1.6384 to 6.5536
- squares_up: float32 [512, 2048], P('fsdp'), may hold values from 1.6384 to 6.5536
- squares_down: float32 [2048, 512], P('fsdp'), may hold values from 1.6384 to 6.5536
- squares_vectors: float32 [8, 512], P(None, 'fsdp'), may hold values from 26.2144 to 104.8576
- squares_bias: float32 [2048], P('fsdp'), may hold values from 0.524288 to 2.097152
Outputs:
- layer_out: bfloat16 [65536, 512], P(('fsdp', 'dp'))
- token_grad: float32 [65536, 512], P(('fsdp', 'dp'))
- grad_norm: float32 [], replicated
- weight_qkv_new: float32 [512, 1536], P('fsdp')
- weight_out_new: float32 [512, 512], P('fsdp')
- weight_up_new: float32 [512, 2048], P('fsdp')
- weight_down_new: float32 [2048, 512], P('fsdp')
- vectors_new: float32 [8, 512], P(None, 'fsdp')
- up_bias_new: float32 [2048], P('fsdp')
- momentum_qkv_new: float32 [512, 1536], P('fsdp')
- momentum_out_new: float32 [512, 512], P('fsdp')
- momentum_up_new: float32 [512, 2048], P('fsdp')
- momentum_down_new: float32 [2048, 512], P('fsdp')
- momentum_vectors_new: float32 [8, 512], P(None, 'fsdp')
- momentum_bias_new: float32 [2048], P('fsdp')
- squares_qkv_new: float32 [512, 1536], P('fsdp')
- squares_out_new: float32 [512, 512], P('fsdp')
- squares_up_new: float32 [512, 2048], P('fsdp')
- squares_down_new: float32 [2048, 512], P('fsdp')
- squares_vectors_new: float32 [8, 512], P(None, 'fsdp')
- squares_bias_new: float32 [2048], P('fsdp')
Inputs may be any that keep to these rules, and one draw needn't show every extreme that they name: `segment_ids`: within a packed sequence the ids number its images 0, 1, 2 and on in order, each image 192 or 384 positions long; positions from the sequence's valid count on hold 5. `valid_counts`: the total length of the images of the sequence, a multiple of 192. `vectors`: rows 0 and 5 are positive.
All inputs are finite; a program needn't handle non-finite values.
Results may differ from a plain program's by a relative error of at most 0.017.
The roundings to bfloat16 on the way count: a program that leaves them out, or rounds other values in their place, can miss the bound.
Values may be sent and summed in bfloat16 or wider, within the bound.
A program may use at most 256 MiB of HBM per device.

v0:
```python
import math

import jax
import jax.numpy as jnp
from jax import lax
from jax.sharding import PartitionSpec as P

D = 512
HEADS = 8
HEAD_DIM = 64
FF = 2048
STEP = 5
PARAMS = 3151872


norm_eps = 1e-06
adam_eps = 1e-08
decay_rate = 0.05
beta_first = 0.5
beta_second = 0.5
masked_score = -1e30


def inner_rows(left, right):
    return lax.dot_general(
        left, right, (((0,), (0,)), ((), ())), preferred_element_type=jnp.float32
    )


def times_transposed(left, right):
    return lax.dot_general(
        left, right, (((1,), (1,)), ((), ())), preferred_element_type=jnp.float32
    )


def norm_forward(values, gain, shift):
    center = values - jnp.mean(values, axis=-1, keepdims=True)
    spread = lax.rsqrt(jnp.mean(center * center, axis=-1, keepdims=True) + norm_eps)
    normed = center * spread
    return (normed * gain + shift, normed, spread)


def norm_backward(incoming, normed, spread, gain):
    scaled = incoming * gain
    return spread * (
        scaled
        - jnp.mean(scaled, axis=-1, keepdims=True)
        - normed * jnp.mean(scaled * normed, axis=-1, keepdims=True)
    )


def gelu_value(values):
    return 0.5 * values * (1.0 + lax.erf(values * (1.0 / math.sqrt(2.0))))


def gelu_slope(values):
    return 0.5 * (1.0 + lax.erf(values * (1.0 / math.sqrt(2.0)))) + values * jnp.exp(
        -0.5 * values * values
    ) * (1.0 / math.sqrt(2.0 * math.pi))


def pair_mask(seg_rows, pos_rows, seg_cols, pos_cols, valid_one):
    same = (seg_rows[:, None] == seg_cols[None, :]) & (pos_cols[None, :] < valid_one)
    return same | (pos_rows[:, None] == pos_cols[None, :])


def split_heads(block_rows):
    return block_rows.reshape(block_rows.shape[0], HEADS, HEAD_DIM)


def attend_forward(qkv_seq, seg_seq, valid_one):
    length = qkv_seq.shape[0]
    block = min(512, length)
    query = split_heads(qkv_seq[:, :D])
    keys = split_heads(qkv_seq[:, D : 2 * D])
    values = split_heads(qkv_seq[:, 2 * D :])
    positions = jnp.arange(length, dtype=jnp.int32)
    factor = 1.0 / math.sqrt(HEAD_DIM)

    def one_block(index):
        start = index * block
        q_rows = lax.dynamic_slice_in_dim(query, start, block, 0)
        seg_rows = lax.dynamic_slice_in_dim(seg_seq, start, block, 0)
        allowed = pair_mask(
            seg_rows, start + jnp.arange(block, dtype=jnp.int32), seg_seq, positions, valid_one
        )
        scores = (
            jnp.einsum("qhd,khd->hqk", q_rows, keys, preferred_element_type=jnp.float32) * factor
        )
        scores = jnp.where(allowed[None], scores, masked_score)
        top = jnp.max(scores, axis=-1, keepdims=True)
        expo = jnp.exp(scores - top)
        total = jnp.sum(expo, axis=-1, keepdims=True)
        probs = (expo / total).astype(jnp.bfloat16)
        mixed = jnp.einsum("hqk,khd->qhd", probs, values, preferred_element_type=jnp.float32)
        return (mixed.reshape(block, D).astype(jnp.bfloat16), (top + jnp.log(total))[:, :, 0])

    mixed, lse = lax.map(one_block, jnp.arange(length // block, dtype=jnp.int32))
    return (mixed.reshape(length, D), lse)


def attend_backward(qkv_seq, grad_seq, lse, seg_seq, valid_one):
    length = qkv_seq.shape[0]
    block = min(512, length)
    query = split_heads(qkv_seq[:, :D])
    keys = split_heads(qkv_seq[:, D : 2 * D])
    values = split_heads(qkv_seq[:, 2 * D :])
    positions = jnp.arange(length, dtype=jnp.int32)
    factor = 1.0 / math.sqrt(HEAD_DIM)

    def one_block(carry, items):
        key_sum, value_sum = carry
        index, block_lse = items
        start = index * block
        q_rows = lax.dynamic_slice_in_dim(query, start, block, 0)
        g_rows = split_heads(lax.dynamic_slice_in_dim(grad_seq, start, block, 0))
        seg_rows = lax.dynamic_slice_in_dim(seg_seq, start, block, 0)
        allowed = pair_mask(
            seg_rows, start + jnp.arange(block, dtype=jnp.int32), seg_seq, positions, valid_one
        )
        scores = (
            jnp.einsum("qhd,khd->hqk", q_rows, keys, preferred_element_type=jnp.float32) * factor
        )
        probs = jnp.where(allowed[None], jnp.exp(scores - block_lse[:, :, None]), 0.0)
        grad_probs = jnp.einsum("qhd,khd->hqk", g_rows, values, preferred_element_type=jnp.float32)
        delta = jnp.sum(probs * grad_probs, axis=-1, keepdims=True)
        grad_scores = (probs * (grad_probs - delta)).astype(jnp.bfloat16)
        grad_query = (
            jnp.einsum("hqk,khd->qhd", grad_scores, keys, preferred_element_type=jnp.float32)
            * factor
        )
        key_sum = (
            key_sum
            + jnp.einsum("hqk,qhd->khd", grad_scores, q_rows, preferred_element_type=jnp.float32)
            * factor
        )
        value_sum = value_sum + jnp.einsum(
            "hqk,qhd->khd", probs.astype(jnp.bfloat16), g_rows, preferred_element_type=jnp.float32
        )
        return ((key_sum, value_sum), grad_query.reshape(block, D))

    zeros = jnp.zeros((length, HEADS, HEAD_DIM), jnp.float32)
    sums, grad_query = lax.scan(
        one_block, (zeros, zeros), (jnp.arange(length // block, dtype=jnp.int32), lse)
    )
    return jnp.concatenate(
        [grad_query.reshape(length, D), sums[0].reshape(length, D), sums[1].reshape(length, D)],
        axis=1,
    )


def adam_step(weight, moment, square, grad, factor, rate):
    clipped = grad * factor
    moment_new = beta_first * moment + (1.0 - beta_first) * clipped
    square_new = beta_second * square + (1.0 - beta_second) * clipped * clipped
    first_hat = moment_new / (1.0 - beta_first**STEP)
    second_hat = square_new / (1.0 - beta_second**STEP)
    weight_new = weight - rate * (
        first_hat / (jnp.sqrt(second_hat) + adam_eps) + decay_rate * weight
    )
    return (weight_new, moment_new, square_new)


def body(
    tokens,
    cotangent,
    segment_ids,
    valid_counts,
    weight_qkv,
    weight_out,
    weight_up,
    weight_down,
    vectors,
    up_bias,
    momentum_qkv,
    momentum_out,
    momentum_up,
    momentum_down,
    momentum_vectors,
    momentum_bias,
    squares_qkv,
    squares_out,
    squares_up,
    squares_down,
    squares_vectors,
    squares_bias,
):
    seqs = valid_counts.shape[0]
    length = segment_ids.shape[1]
    rows_local = tokens.shape[0]
    wide = lax.axis_size("fsdp")
    replicas = lax.axis_size("dp")
    low_qkv = weight_qkv.astype(jnp.bfloat16)
    low_out = weight_out.astype(jnp.bfloat16)
    low_up = weight_up.astype(jnp.bfloat16)
    low_down = weight_down.astype(jnp.bfloat16)
    low_vectors = vectors.astype(jnp.bfloat16)
    low_bias = up_bias.astype(jnp.bfloat16)
    full_qkv, full_out, full_up, full_down, full_vectors, full_bias = (
        lax.all_gather(low_qkv, "fsdp", axis=0, tiled=True),
        lax.all_gather(low_out, "fsdp", axis=0, tiled=True),
        lax.all_gather(low_up, "fsdp", axis=0, tiled=True),
        lax.all_gather(low_down, "fsdp", axis=0, tiled=True),
        lax.all_gather(low_vectors, "fsdp", axis=1, tiled=True),
        lax.all_gather(low_bias, "fsdp", axis=0, tiled=True),
    )
    vector_rows = full_vectors.astype(jnp.float32)
    bias_rows = full_bias.astype(jnp.float32)
    rows = tokens.astype(jnp.float32)
    normed_one, hat_one, spread_one = norm_forward(rows, vector_rows[0], vector_rows[1])
    low_one = normed_one.astype(jnp.bfloat16)
    qkv_bias = jnp.concatenate([vector_rows[2], jnp.zeros((D,), jnp.float32), vector_rows[3]])
    qkv_low = (jnp.dot(low_one, full_qkv, preferred_element_type=jnp.float32) + qkv_bias).astype(
        jnp.bfloat16
    )
    qkv_seqs = qkv_low.reshape(seqs, length, 3 * D)

    def forward_sequence(items):
        return attend_forward(items[0], items[1], items[2])

    mixed, lse = lax.map(forward_sequence, (qkv_seqs, segment_ids, valid_counts))
    attended = mixed.reshape(rows_local, D)
    resid = rows + (
        jnp.dot(attended, full_out, preferred_element_type=jnp.float32) + vector_rows[4]
    )
    normed_two, hat_two, spread_two = norm_forward(resid, vector_rows[5], vector_rows[6])
    low_two = normed_two.astype(jnp.bfloat16)
    hidden = jnp.dot(low_two, full_up, preferred_element_type=jnp.float32) + bias_rows
    active = gelu_value(hidden).astype(jnp.bfloat16)
    layer_out = (
        resid + (jnp.dot(active, full_down, preferred_element_type=jnp.float32) + vector_rows[7])
    ).astype(jnp.bfloat16)
    live = (
        (jnp.arange(length, dtype=jnp.int32)[None, :] < valid_counts[:, None])
        .astype(jnp.float32)
        .reshape(rows_local, 1)
    )
    grad_out = cotangent.astype(jnp.float32) * live
    back_qkv, back_out, back_up, back_down, back_vectors = (
        lax.all_gather(low_qkv, "fsdp", axis=0, tiled=True),
        lax.all_gather(low_out, "fsdp", axis=0, tiled=True),
        lax.all_gather(low_up, "fsdp", axis=0, tiled=True),
        lax.all_gather(low_down, "fsdp", axis=0, tiled=True),
        lax.all_gather(low_vectors, "fsdp", axis=1, tiled=True),
    )
    back_rows = back_vectors.astype(jnp.float32)
    grad_out_low = grad_out.astype(jnp.bfloat16)
    grad_w_down = inner_rows(active, grad_out_low)
    grad_active = times_transposed(grad_out_low, back_down)
    grad_hidden = grad_active * gelu_slope(hidden)
    grad_hidden_low = grad_hidden.astype(jnp.bfloat16)
    grad_w_up = inner_rows(low_two, grad_hidden_low)
    grad_low_two = times_transposed(grad_hidden_low, back_up)
    grad_resid = grad_out + norm_backward(grad_low_two, hat_two, spread_two, back_rows[5])
    grad_resid_low = grad_resid.astype(jnp.bfloat16)
    grad_w_out = inner_rows(attended, grad_resid_low)
    grad_attended = times_transposed(grad_resid_low, back_out).astype(jnp.bfloat16)
    grad_seqs = grad_attended.reshape(seqs, length, D)

    def backward_sequence(items):
        return attend_backward(items[0], items[1], items[2], items[3], items[4])

    grad_qkv = lax.map(
        backward_sequence, (qkv_seqs, grad_seqs, lse, segment_ids, valid_counts)
    ).reshape(rows_local, 3 * D)
    grad_qkv_low = grad_qkv.astype(jnp.bfloat16)
    grad_w_qkv = inner_rows(low_one, grad_qkv_low)
    grad_low_one = times_transposed(grad_qkv_low, back_qkv)
    token_grad = grad_resid + norm_backward(grad_low_one, hat_one, spread_one, back_rows[0])
    grad_vectors = jnp.stack(
        [
            jnp.sum(grad_low_one * hat_one, axis=0),
            jnp.sum(grad_low_one, axis=0),
            jnp.sum(grad_qkv[:, :D], axis=0),
            jnp.sum(grad_qkv[:, 2 * D :], axis=0),
            jnp.sum(grad_resid, axis=0),
            jnp.sum(grad_low_two * hat_two, axis=0),
            jnp.sum(grad_low_two, axis=0),
            jnp.sum(grad_out, axis=0),
        ]
    )
    grad_bias_up = jnp.sum(grad_hidden, axis=0)
    shards = (
        lax.psum_scatter(grad_w_qkv, "fsdp", scatter_dimension=0, tiled=True),
        lax.psum_scatter(grad_w_out, "fsdp", scatter_dimension=0, tiled=True),
        lax.psum_scatter(grad_w_up, "fsdp", scatter_dimension=0, tiled=True),
        lax.psum_scatter(grad_w_down, "fsdp", scatter_dimension=0, tiled=True),
        lax.psum_scatter(grad_vectors, "fsdp", scatter_dimension=1, tiled=True),
        lax.psum_scatter(grad_bias_up, "fsdp", scatter_dimension=0, tiled=True),
    )
    grads = (
        lax.psum(shards[0].astype(jnp.bfloat16), "dp").astype(jnp.float32),
        lax.psum(shards[1].astype(jnp.bfloat16), "dp").astype(jnp.float32),
        lax.psum(shards[2].astype(jnp.bfloat16), "dp").astype(jnp.float32),
        lax.psum(shards[3].astype(jnp.bfloat16), "dp").astype(jnp.float32),
        lax.psum(shards[4].astype(jnp.bfloat16), "dp").astype(jnp.float32),
        lax.psum(shards[5].astype(jnp.bfloat16), "dp").astype(jnp.float32),
    )
    local_total = jnp.sum(grads[0] * grads[0])
    for item in grads[1:]:
        local_total = local_total + jnp.sum(item * item)
    grad_norm = jnp.sqrt(lax.psum(local_total, "fsdp"))
    bound = 0.005 * math.sqrt(rows_local * wide * replicas * PARAMS)
    factor = jnp.minimum(1.0, bound / grad_norm)
    rates = (
        2.0 / math.sqrt(D),
        8.0 / math.sqrt(D),
        2.0 / math.sqrt(D),
        2.0 / math.sqrt(FF),
        0.5,
        0.5,
    )
    masters = (weight_qkv, weight_out, weight_up, weight_down, vectors, up_bias)
    moments = (
        momentum_qkv,
        momentum_out,
        momentum_up,
        momentum_down,
        momentum_vectors,
        momentum_bias,
    )
    squares = (squares_qkv, squares_out, squares_up, squares_down, squares_vectors, squares_bias)
    fresh = [
        adam_step(masters[k], moments[k], squares[k], grads[k], factor, rates[k]) for k in range(6)
    ]
    return (
        layer_out,
        token_grad,
        grad_norm,
        fresh[0][0],
        fresh[1][0],
        fresh[2][0],
        fresh[3][0],
        fresh[4][0],
        fresh[5][0],
        fresh[0][1],
        fresh[1][1],
        fresh[2][1],
        fresh[3][1],
        fresh[4][1],
        fresh[5][1],
        fresh[0][2],
        fresh[1][2],
        fresh[2][2],
        fresh[3][2],
        fresh[4][2],
        fresh[5][2],
    )


def solution(mesh):
    placed = (
        P(("fsdp", "dp"), None),
        P(("fsdp", "dp"), None),
        P(("fsdp", "dp"), None),
        P(("fsdp", "dp")),
        P("fsdp", None),
        P("fsdp", None),
        P("fsdp", None),
        P("fsdp", None),
        P(None, "fsdp"),
        P("fsdp"),
        P("fsdp", None),
        P("fsdp", None),
        P("fsdp", None),
        P("fsdp", None),
        P(None, "fsdp"),
        P("fsdp"),
        P("fsdp", None),
        P("fsdp", None),
        P("fsdp", None),
        P("fsdp", None),
        P(None, "fsdp"),
        P("fsdp"),
    )
    return jax.shard_map(
        body,
        mesh=mesh,
        in_specs=placed,
        out_specs=(
            P(("fsdp", "dp"), None),
            P(("fsdp", "dp"), None),
            P(),
            P("fsdp", None),
            P("fsdp", None),
            P("fsdp", None),
            P("fsdp", None),
            P(None, "fsdp"),
            P("fsdp"),
            P("fsdp", None),
            P("fsdp", None),
            P("fsdp", None),
            P("fsdp", None),
            P(None, "fsdp"),
            P("fsdp"),
            P("fsdp", None),
            P("fsdp", None),
            P("fsdp", None),
            P("fsdp", None),
            P(None, "fsdp"),
            P("fsdp"),
        ),
        check_vma=False,
    )
```

profile of v0, /device:TPU:0, one launch (start us, length us, event | category | flops | bytes accessed | tf_op | source)
XLA Modules:
  0.0 1200.9 jit_solution(5182117981191907554)
XLA Ops:
  13.7 42.2 %all-gather.1 = bf16[16,1,128]{2,1,0:T(2,128)(2,1)S(1)} all-gather(bf16[1,1,128]{2,1,0:T(2,128)(2,1)S(1)} %convert_bitcast_fusion.1), channel_id=1, replica_groups=mesh['fsdp'=16,'dp'=2] {'fsdp'}, dimensions={0}, use_global_device_ids=true | all-gather | bytes 4352 | tf_op jit(solution)/shard_map/all_gather | solution.py:205
  57.8 35.7 %all-gather = bf16[16,32,8]{1,2,0:T(8,128)(2,1)S(1)} all-gather(bf16[1,32,8]{1,2,0:T(8,128)(2,1)S(1)} %convert_bitcast_fusion), channel_id=1, replica_groups=mesh['fsdp'=16,'dp'=2] {'fsdp'}, dimensions={0}, use_global_device_ids=true | all-gather | bytes 8704 | tf_op jit(solution)/shard_map/all_gather | solution.py:204
  95.1 44.9 %all_gather.25 = bf16[512,512]{1,0:T(8,128)(2,1)} all-gather(bf16[32,512]{1,0:T(8,128)(2,1)S(1)} %convert_element_type.138), channel_id=1, replica_groups=mesh['fsdp'=16,'dp'=2] {'fsdp'}, dimensions={0}, use_global_device_ids=true | all-gather | bytes 557056 | tf_op jit(solution)/shard_map/all_gather | solution.py:201
  163.8 80.6 %while.53 = (s32[]{:T(128)}, bf16[2,1024,512]{2,1,0:T(8,128)(2,1)}, f32[2,2,8,512]{3,2,1,0:T(8,128)}, bf16[2,1024,1536]{1,2,0:T(8,128)(2,1)}, s32[2,1024]{1,0:T(...) while((s32[]{:T(128)}, bf16[2,1024,512]{2,1,0:T(8,128)(2,1)}, ...), condition=%wide.region_7.8_spmd, body=%wide.region_2.7_spmd.sunk | while | flops 1126430208 | bytes 77292080 | solution.py:221
  169.3 32.3 %while.56 = (s32[]{:T(128)}, bf16[2,512,512]{2,1,0:T(8,128)(2,1)}, f32[2,8,512]{2,1,0:T(8,128)S(1)}, s32[2]{0:T(128)S(1)}, s32[1024]{0:T(1024)S(1)}, /*index=5*/...) while((s32[]{:T(128)}, bf16[2,512,512]{2,1,0:T(8,128)(2,1)}, ...), condition=%wide.region_6.6_spmd.clone.clone, body=%wide.region_3.5_spmd.clone.clone.sunk | while | flops 1126430208 | bytes 62013680 | solution.py:98
  209.4 32.3 %while.56 = (s32[]{:T(128)}, bf16[2,512,512]{2,1,0:T(8,128)(2,1)}, f32[2,8,512]{2,1,0:T(8,128)S(1)}, s32[2]{0:T(128)S(1)}, s32[1024]{0:T(1024)S(1)}, /*index=5*/...) while((s32[]{:T(128)}, bf16[2,512,512]{2,1,0:T(8,128)(2,1)}, ...), condition=%wide.region_6.6_spmd.clone.clone, body=%wide.region_3.5_spmd.clone.clone.sunk | while | flops 1126430208 | bytes 62013680 | solution.py:98
  251.0 13.2 %multiply_convert_fusion.1 = (bf16[2048,2048]{1,0:T(8,128)(2,1)}, f32[2048,2048]{1,0:T(8,128)}) fusion(f32[2048]{0:T(1024)S(1)} %bitcast.226, bf16[512,2048]{1,0:T(8,128)(2,1)} %all-gather.8.cloned.1.call-done, f32[2048,512]{0,1:T(8,128)} %copy-done.11, f32[512]{0:T(512)S(1)} %bitcast.232, f32[512]{0:T(512)S(1)} %bitcast.212, f32[2048]{0:T(1024)S(1)} %add_rsqrt_fusion, ...), kind=kOutput, calls=%fused_computation.54 | convolution fusion | flops 4325376000 | bytes 31485952 | tf_op jit(solution)/shard_map/dot_general | solution.py:228
  264.3 13.6 %fusion.86 = (f32[2048]{0:T(1024)}, bf16[2048,2048]{1,0:T(8,128)(2,1)S(1)}) fusion(f32[2048,2048]{1,0:T(8,128)} %get-tuple-element.563, f32[2048]{0:T(1024)S(1)} %bitcast.227, bf16[2048,512]{1,0:T(8,128)(2,1)} %all-gather.10.cloned.1.call-done, bf16[2048,512]{0,1:T(8,128)(2,1)S(1)} %copy-done.17, f32[2048]{0:T(1024)S(1)} %bitcast.209), kind=kOutput, calls=%fused_computation.165 | convolution fusion | flops 4348442624 | bytes 29384704 | tf_op jit(solution)/shard_map/dot_general | solution.py:31
  301.2 309.4 %while.55 = (s32[]{:T(128)}, f32[2,1024,1536]{2,1,0:T(8,128)}, f32[2,2,8,512]{3,2,1,0:T(8,128)}, bf16[2,1024,1536]{1,2,0:T(8,128)(2,1)}, bf16[2,1024,512]{2,1,0:...) while((s32[]{:T(128)}, f32[2,1024,1536]{2,1,0:T(8,128)}, ...), condition=%wide.region_16.17_spmd, body=%wide.region_12.16_spmd.sunk | while | flops 2730227200 | bytes 289841984 | solution.py:263
  309.5 126.6 %while.57 = (s32[]{:T(128)}, f32[1024,8,64]{0,2,1:T(8,128)}, f32[1024,8,64]{0,2,1:T(8,128)}, f32[2,512,512]{1,0,2:T(2,128)}, s32[2]{0:T(128)S(1)}, /*index=5*/bf...) while((s32[]{:T(128)}, f32[1024,8,64]{0,2,1:T(8,128)}, ...), condition=%wide.region_15.15_spmd.clone.clone, body=%wide.region_13.14_spmd.clone.clone.sunk | while | flops 2727081472 | bytes 205881808 | solution.py:143
  317.4 11.7 multiply_reduce_fusion.8
  353.0 19.5 %dynamic_update_slice.44 = f32[2,512,512]{1,0,2:T(2,128)} dynamic-update-slice(f32[2,512,512]{1,0,2:T(2,128)} %get-tuple-element.875, f32[1,512,512]{1,0,2:T(1,128)S(1)} %copy.134, s32[]{:T(128)S(6)} %copy.141, s32[]{:T(128)} %constant.73.clone.1..sunk.3..sunk, s32[]{:T(128)} %constant.73.clone.1..sunk.3..sunk) | dynamic-update-slice | bytes 2097156 | tf_op jit(solution)/shard_map/while/body/eval_jaxpr/while/body/jit(dynamic_update_index_in_dim)/dynamic_update_slice | solution.py:143
  380.5 11.7 multiply_reduce_fusion.8
  401.4 9.5 bitcast_add_fusion.5
  416.6 19.5 %dynamic_update_slice.44 = f32[2,512,512]{1,0,2:T(2,128)} dynamic-update-slice(f32[2,512,512]{1,0,2:T(2,128)} %get-tuple-element.875, f32[1,512,512]{1,0,2:T(1,128)S(1)} %copy.134, s32[]{:T(128)S(6)} %copy.141, s32[]{:T(128)} %constant.73.clone.1..sunk.3..sunk, s32[]{:T(128)} %constant.73.clone.1..sunk.3..sunk) | dynamic-update-slice | bytes 2097156 | tf_op jit(solution)/shard_map/while/body/eval_jaxpr/while/body/jit(dynamic_update_index_in_dim)/dynamic_update_slice | solution.py:143
  464.0 126.6 %while.57 = (s32[]{:T(128)}, f32[1024,8,64]{0,2,1:T(8,128)}, f32[1024,8,64]{0,2,1:T(8,128)}, f32[2,512,512]{1,0,2:T(2,128)}, s32[2]{0:T(128)S(1)}, /*index=5*/bf...) while((s32[]{:T(128)}, f32[1024,8,64]{0,2,1:T(8,128)}, ...), condition=%wide.region_15.15_spmd.clone.clone, body=%wide.region_13.14_spmd.clone.clone.sunk | while | flops 2727081472 | bytes 205881808 | solution.py:143
  472.0 11.7 multiply_reduce_fusion.8
  507.6 19.5 %dynamic_update_slice.44 = f32[2,512,512]{1,0,2:T(2,128)} dynamic-update-slice(f32[2,512,512]{1,0,2:T(2,128)} %get-tuple-element.875, f32[1,512,512]{1,0,2:T(1,128)S(1)} %copy.134, s32[]{:T(128)S(6)} %copy.141, s32[]{:T(128)} %constant.73.clone.1..sunk.3..sunk, s32[]{:T(128)} %constant.73.clone.1..sunk.3..sunk) | dynamic-update-slice | bytes 2097156 | tf_op jit(solution)/shard_map/while/body/eval_jaxpr/while/body/jit(dynamic_update_index_in_dim)/dynamic_update_slice | solution.py:143
  535.0 11.7 multiply_reduce_fusion.8
  571.2 19.5 %dynamic_update_slice.44 = f32[2,512,512]{1,0,2:T(2,128)} dynamic-update-slice(f32[2,512,512]{1,0,2:T(2,128)} %get-tuple-element.875, f32[1,512,512]{1,0,2:T(1,128)S(1)} %copy.134, s32[]{:T(128)S(6)} %copy.141, s32[]{:T(128)} %constant.73.clone.1..sunk.3..sunk, s32[]{:T(128)} %constant.73.clone.1..sunk.3..sunk) | dynamic-update-slice | bytes 2097156 | tf_op jit(solution)/shard_map/while/body/eval_jaxpr/while/body/jit(dynamic_update_index_in_dim)/dynamic_update_slice | solution.py:143
  614.8 9.7 fusion.84
  640.0 9.7 fusion.48
  650.1 10.7 fusion.52
  661.5 11.2 fusion.42
  674.7 11.2 add_convert_fusion.1
  689.8 37.2 %all-reduce = bf16[2048]{0:T(1024)(128)(2,1)S(1)} all-reduce(f32[2048]{0:T(1024)S(1)} %copy-done.53), channel_id=7, replica_groups=mesh['fsdp'=16,'dp'=2] {'fsdp'}, use_global_device_ids=true, to_apply=%region_43.44.clone | all-reduce | flops 2048 | bytes 12288
  735.0 48.1 %reduce-scatter.10.cloned.1.call-done = f32[32,512]{1,0:T(8,128)} async-done(((f32[512,512]{1,0:T(8,128)}), f32[32,512]{1,0:T(8,128)}) %reduce-scatter.10.cloned.1.call-update) | async-done | bytes 65552 | tf_op jit(solution)/shard_map/reduce_scatter | solution.py:285
  784.0 131.0 %reduce-scatter.8.cloned.1.call-done = f32[32,1536]{1,0:T(8,128)} async-done(((f32[512,1536]{1,0:T(8,128)}), f32[32,1536]{1,0:T(8,128)}) %reduce-scatter.8.cloned.1.call-update) | async-done | bytes 196624 | tf_op jit(solution)/shard_map/reduce_scatter | solution.py:284
  916.5 95.1 %reduce-scatter.14.cloned.1.call-done = f32[128,512]{1,0:T(8,128)} async-done(((f32[2048,512]{1,0:T(8,128)}), f32[128,512]{1,0:T(8,128)}) %reduce-scatter.14.cloned.1.call-update) | async-done | bytes 262160 | tf_op jit(solution)/shard_map/reduce_scatter | solution.py:287
  1013.2 95.4 %reduce-scatter.12.cloned.1.call-done = f32[32,2048]{1,0:T(8,128)} async-done(((f32[512,2048]{1,0:T(8,128)}), f32[32,2048]{1,0:T(8,128)}) %reduce-scatter.12.cloned.1.call-update) | async-done | bytes 262160 | tf_op jit(solution)/shard_map/reduce_scatter | solution.py:286
  1115.6 14.9 %all-reduce.5.cloned.1.call-done = (bf16[32,1536]{1,0:T(8,128)(2,1)}, bf16[32,2048]{1,0:T(8,128)(2,1)}, bf16[128,512]{1,0:T(8,128)(2,1)}) async-done(((bf16[32,1536]{1,0:T(8,128)(2,1)}, bf16[32,2048]{1,0:T(8,128)(2,1)}, bf16[128,512]{1,0:T(8,128)(2,1)}), (bf16[32,1536]{1,0:T(8,128)(2,1)}, bf16[32,2048]{1,0:T(8,128)(2,1)}, bf16[128,512]{1,0:T(8,128)(2,1)})) %all-reduce.5.cloned.1.call-update) | async-done | bytes 360464 | tf_op jit(solution)/shard_map/psum | solution.py:292
  1144.9 42.5 %psum.55 = f32[]{:T(128)} all-reduce(f32[]{:T(128)S(6)} %add.312), channel_id=1, replica_groups=mesh['fsdp'=16,'dp'=2] {'fsdp'}, use_global_device_ids=true, to_apply=%region_46.47 | all-reduce | flops 1 | bytes 8 | tf_op jit(solution)/shard_map/psum | solution.py:302
  (433 shorter events, 372.6 us)
Async XLA Ops:
  7.2 140.8 %all-gather.6.cloned.1.call-start = ((), (), s32[]{:S(2)}) async-start(), calls=%async_computation.5 | async-start | bytes 1671168 | tf_op jit(solution)/shard_map/all_gather | solution.py:200
  8.8 242.1 %all-gather.8.cloned.1.call-start = ((), (), s32[]{:S(2)}) async-start(), calls=%async_computation.6 | async-start | bytes 2228224 | tf_op jit(solution)/shard_map/all_gather | solution.py:202
  10.5 253.7 %all-gather.10.cloned.1.call-start = ((), (), s32[]{:S(2)}) async-start(), calls=%async_computation.7 | async-start | bytes 2228224 | tf_op jit(solution)/shard_map/all_gather | solution.py:203
  12.2 722.0 %reduce-scatter.16.cloned.1.call-start = ((), (), s32[]{:S(2)}) async-start(), calls=%async_computation.12 | async-start | bytes 278528
  94.2 53.7 %copy-start.48 = (f32[1,512]{1,0:T(1,128)}, f32[1,512]{1,0:T(1,128)S(1)}, u32[]{:S(2)}) copy-start(f32[1,512]{1,0:T(1,128)S(1)} %get-tuple-element.559) | copy-start | bytes 6148
  94.2 53.7 %copy-start.61 = (f32[1,512]{1,0:T(1,128)}, f32[1,512]{1,0:T(1,128)S(1)}, u32[]{:S(2)}) copy-start(f32[1,512]{1,0:T(1,128)S(1)} %get-tuple-element.558) | copy-start | bytes 6148
  163.8 80.6 %copy-start.64 = (f32[1,512]{1,0:T(1,128)S(1)}, f32[1,512]{1,0:T(1,128)}, u32[]{:S(2)}) copy-start(f32[1,512]{1,0:T(1,128)} %get-tuple-element.555) | copy-start | bytes 6148
  634.7 148.4 %reduce-scatter.10.cloned.1.call-start = ((), (), s32[]{:S(2)}) async-start(), calls=%async_computation.9 | async-start | bytes 1114112 | tf_op jit(solution)/shard_map/reduce_scatter | solution.py:285
  639.9 275.0 %reduce-scatter.8.cloned.1.call-start = ((), (), s32[]{:S(2)}) async-start(), calls=%async_computation.8 | async-start | bytes 3342336 | tf_op jit(solution)/shard_map/reduce_scatter | solution.py:284
  649.7 361.9 %reduce-scatter.14.cloned.1.call-start = ((), (), s32[]{:S(2)}) async-start(), calls=%async_computation.11 | async-start | bytes 4456448 | tf_op jit(solution)/shard_map/reduce_scatter | solution.py:287
  660.8 447.8 %reduce-scatter.12.cloned.1.call-start = ((), (), s32[]{:S(2)}) async-start(), calls=%async_computation.10 | async-start | bytes 4456448 | tf_op jit(solution)/shard_map/reduce_scatter | solution.py:286
  672.8 457.7 %all-reduce.5.cloned.1.call-start = ((), (), s32[]{:S(2)}) async-start(), calls=%async_computation.13 | async-start | bytes 720896 | tf_op jit(solution)/shard_map/psum | solution.py:292
  1139.1 49.1 %copy-start.65 = (f32[128]{0:T(128)S(1)}, f32[128]{0:T(128)}, u32[]{:S(2)}) copy-start(f32[128]{0:T(128)} %param.39) | copy-start | bytes 1540
  1139.1 49.1 %copy-start.66 = (f32[128]{0:T(128)S(1)}, f32[128]{0:T(128)}, u32[]{:S(2)}) copy-start(f32[128]{0:T(128)} %param.45) | copy-start | bytes 1540
  1139.1 49.6 %copy-start.50 = (f32[8,32]{1,0:T(8,128)S(1)}, f32[8,32]{1,0:T(8,128)}, u32[]{:S(2)}) copy-start(f32[8,32]{1,0:T(8,128)} %param.38) | copy-start | bytes 3076
  1139.1 49.6 %copy-start.56 = (f32[8,32]{1,0:T(8,128)S(1)}, f32[8,32]{1,0:T(8,128)}, u32[]{:S(2)}) copy-start(f32[8,32]{1,0:T(8,128)} %param.44) | copy-start | bytes 3076
  1139.2 49.6 %copy-start.57 = (f32[8,32]{1,0:T(8,128)S(1)}, f32[8,32]{1,0:T(8,128)}, u32[]{:S(2)}) copy-start(f32[8,32]{1,0:T(8,128)} %param.50) | copy-start | bytes 3076
  1139.2 50.2 %copy-start.31 = (f32[32,512]{1,0:T(8,128)S(1)}, f32[32,512]{1,0:T(8,128)}, u32[]{:S(2)}) copy-start(f32[32,512]{1,0:T(8,128)} %param.35) | copy-start | bytes 196612
  1139.2 50.2 %copy-start.42 = (f32[32,512]{1,0:T(8,128)S(1)}, f32[32,512]{1,0:T(8,128)}, u32[]{:S(2)}) copy-start(f32[32,512]{1,0:T(8,128)} %param.41) | copy-start | bytes 196612
  1139.2 50.2 %copy-start.43 = (f32[32,512]{1,0:T(8,128)S(1)}, f32[32,512]{1,0:T(8,128)}, u32[]{:S(2)}) copy-start(f32[32,512]{1,0:T(8,128)} %param.47) | copy-start | bytes 196612
  1139.2 50.9 %copy-start.21 = (f32[32,1536]{1,0:T(8,128)S(1)}, f32[32,1536]{1,0:T(8,128)}, u32[]{:S(2)}) copy-start(f32[32,1536]{1,0:T(8,128)} %param.34) | copy-start | bytes 589828
  1139.2 50.9 %copy-start.26 = (bf16[32,1536]{1,0:T(8,128)(2,1)S(1)}, bf16[32,1536]{1,0:T(8,128)(2,1)}, u32[]{:S(2)}) copy-start(bf16[32,1536]{1,0:T(8,128)(2,1)} %get-tuple-element.518) | copy-start | bytes 294916
  1139.2 50.9 %copy-start.32 = (f32[32,1536]{1,0:T(8,128)S(1)}, f32[32,1536]{1,0:T(8,128)}, u32[]{:S(2)}) copy-start(f32[32,1536]{1,0:T(8,128)} %param.40) | copy-start | bytes 589828
  1139.2 50.8 %copy-start.33 = (f32[32,1536]{1,0:T(8,128)S(1)}, f32[32,1536]{1,0:T(8,128)}, u32[]{:S(2)}) copy-start(f32[32,1536]{1,0:T(8,128)} %param.46) | copy-start | bytes 589828
  1139.2 51.8 %copy-start.19 = (f32[128,512]{1,0:T(8,128)S(1)}, f32[128,512]{1,0:T(8,128)}, u32[]{:S(2)}) copy-start(f32[128,512]{1,0:T(8,128)} %param.37) | copy-start | bytes 786436
  1139.3 51.7 %copy-start.23 = (bf16[128,512]{1,0:T(8,128)(2,1)S(1)}, bf16[128,512]{1,0:T(8,128)(2,1)}, u32[]{:S(2)}) copy-start(bf16[128,512]{1,0:T(8,128)(2,1)} %get-tuple-element.520) | copy-start | bytes 393220
  1139.3 51.7 %copy-start.27 = (f32[128,512]{1,0:T(8,128)S(1)}, f32[128,512]{1,0:T(8,128)}, u32[]{:S(2)}) copy-start(f32[128,512]{1,0:T(8,128)} %param.43) | copy-start | bytes 786436
  1139.3 51.7 %copy-start.28 = (f32[128,512]{1,0:T(8,128)S(1)}, f32[128,512]{1,0:T(8,128)}, u32[]{:S(2)}) copy-start(f32[128,512]{1,0:T(8,128)} %param.49) | copy-start | bytes 786436
  1139.3 52.8 %copy-start.20 = (f32[32,2048]{1,0:T(8,128)S(1)}, f32[32,2048]{1,0:T(8,128)}, u32[]{:S(2)}) copy-start(f32[32,2048]{1,0:T(8,128)} %param.36) | copy-start | bytes 786436
  1139.3 52.8 %copy-start.22 = (bf16[32,2048]{1,0:T(8,128)(2,1)S(1)}, bf16[32,2048]{1,0:T(8,128)(2,1)}, u32[]{:S(2)}) copy-start(bf16[32,2048]{1,0:T(8,128)(2,1)} %get-tuple-element.519) | copy-start | bytes 393220
  1139.3 52.7 %copy-start.29 = (f32[32,2048]{1,0:T(8,128)S(1)}, f32[32,2048]{1,0:T(8,128)}, u32[]{:S(2)}) copy-start(f32[32,2048]{1,0:T(8,128)} %param.42) | copy-start | bytes 786436
  1139.3 52.7 %copy-start.30 = (f32[32,2048]{1,0:T(8,128)S(1)}, f32[32,2048]{1,0:T(8,128)}, u32[]{:S(2)}) copy-start(f32[32,2048]{1,0:T(8,128)} %param.48) | copy-start | bytes 786436
  (78 other events, 692.1 us)
Sparse Core Ops, SparseCore 0:
  11.4 60.5 all-gather.5
  75.3 61.6 all-gather.7
  140.3 59.6 all-gather.9
  634.8 71.9 reduce-scatter.15
  709.0 74.0 reduce-scatter.9
  787.9 126.9 reduce-scatter.7
  917.2 94.3 reduce-scatter.13
  1013.9 94.7 reduce-scatter.11
  1112.3 18.1 all-reduce.4
where the time goes:
time: 1220 us; the launch traced here: 1200 us
  waiting for transfers between devices  385 us (32%)
  matrix products  252 us (21%)
  blocking collectives  206 us (17%)
  local copies, waits for them, and re-layouts  204 us (17%)
  other arithmetic  125 us (10%)
  between operations  21.1 us (2%)
    reduce_scatter x1, waiting for transfers between devices, body(): lax.psum_scatter(grad_w_qkv, 'fsdp', scatter_dimension=0, tiled=True)  131 us
    reduce_scatter x1, waiting for transfers between devices, body(): lax.psum_scatter(grad_w_up, 'fsdp', scatter_dimension=0, tiled=True)  95.4 us
    reduce_scatter x1, waiting for transfers between devices, body(): lax.psum_scatter(grad_w_down, 'fsdp', scatter_dimension=0, tiled=True)  95.1 us
    dynamic_update_slice x8, local copies, waits for them, and re-layouts, attend_backward(): lax.scan(one_block, (zeros, zeros), (jnp.arange(length // block, dtype=jn...  82.2 us
    dot_general x8, matrix products, one_block(): jnp.einsum('qhd,khd->hqk', q_rows, keys, preferred_element_type=jnp.float32)  58.7 us
    reduce_scatter x1, waiting for transfers between devices, body(): lax.psum_scatter(grad_w_out, 'fsdp', scatter_dimension=0, tiled=True)  48.1 us
    all_gather x1, blocking collectives, body(): lax.all_gather(low_out, 'fsdp', axis=0, tiled=True)  44.9 us
    psum x1, blocking collectives, body(): grad_norm = jnp.sqrt(lax.psum(local_total, 'fsdp'))  42.5 us
  transfers between devices with their start and end apart: 9, of which 5 were waited for; matrix products, arithmetic and copies ran while one was open for 16% of the time, Pallas kernels for 0%

commit v1 on v0

v1 whole, which is shorter than its diff:
```python
import functools
import math

import jax
import jax.numpy as jnp
from jax import lax
from jax.experimental import pallas as pl
from jax.experimental.pallas import tpu as pltpu
from jax.sharding import PartitionSpec as P

D = 512
HEADS = 8
HEAD_DIM = 64
FF = 2048
SEQ = 1024
IMG = 192
BLOCKS = 5
STEP = 5
PARAMS = 3151872
GROUP = 256
PER_GROUP = GROUP // HEAD_DIM

F32 = jnp.float32
BF16 = jnp.bfloat16

norm_eps = 1e-06
adam_eps = 1e-08
decay_rate = 0.05
beta_first = 0.5
beta_second = 0.5
masked_score = -1e30


def dot(left, right):
    return lax.dot_general(left, right, (((1,), (0,)), ((), ())), preferred_element_type=F32)


def dot_nt(left, right):
    return lax.dot_general(left, right, (((1,), (1,)), ((), ())), preferred_element_type=F32)


def dot_tn(left, right):
    return lax.dot_general(left, right, (((0,), (0,)), ((), ())), preferred_element_type=F32)


def norm_forward(values, gain, shift):
    center = values - jnp.mean(values, axis=-1, keepdims=True)
    spread = lax.rsqrt(jnp.mean(center * center, axis=-1, keepdims=True) + norm_eps)
    hat = center * spread
    return hat * gain + shift, hat, spread


def norm_backward(incoming, hat, spread, gain):
    scaled = incoming * gain
    return spread * (
        scaled
        - jnp.mean(scaled, axis=-1, keepdims=True)
        - hat * jnp.mean(scaled * hat, axis=-1, keepdims=True)
    )


def gelu_pair(values):
    half = 0.5 * (1.0 + lax.erf(values * (1.0 / math.sqrt(2.0))))
    bell = jnp.exp(-0.5 * values * values) * (1.0 / math.sqrt(2.0 * math.pi))
    return values * half, half + values * bell


def col_sum(values):
    return jnp.sum(values, axis=0, keepdims=True)


def head_of_lane():
    return lax.broadcasted_iota(jnp.int32, (1, GROUP), 1) // HEAD_DIM


def stack_heads(rows):
    head = head_of_lane()
    zero = jnp.zeros_like(rows)
    return jnp.concatenate([jnp.where(head == h, rows, zero) for h in range(PER_GROUP)], axis=0)


def unstack_heads(stacked):
    head = head_of_lane()
    n = stacked.shape[0] // PER_GROUP
    rows = stacked[(PER_GROUP - 1) * n :]
    for h in range(PER_GROUP - 2, -1, -1):
        rows = jnp.where(head == h, stacked[h * n : (h + 1) * n], rows)
    return rows


def links(seg, counts, s):
    return [
        (seg[s, b * IMG] == seg[s, (b + 1) * IMG]) & ((b + 1) * IMG < counts[s])
        for b in range(BLOCKS - 1)
    ]


def neighbour(b, linked):
    below = slice((b + 1) * IMG, (b + 2) * IMG) if b < BLOCKS - 1 else None
    above = slice((b - 1) * IMG, b * IMG) if b > 0 else None
    with_below = linked[b] if b < BLOCKS - 1 else jnp.bool_(False)
    with_above = linked[b - 1] if b > 0 else jnp.bool_(False)
    offset = jnp.where(with_below | with_above, 0.0, masked_score)
    return below, above, with_below, with_above, offset


def other_rows(ref, cols, below, above, with_below):
    if above is None:
        return ref[below, cols]
    if below is None:
        return ref[above, cols]
    return jnp.where(with_below, ref[below, cols], ref[above, cols])


def attend_block(query, keys, values, offset):
    stacked = stack_heads(query * jnp.asarray(HEAD_DIM**-0.5, BF16))
    scores = dot_nt(keys, stacked)
    own, other = scores[:IMG], scores[IMG:]
    top = jnp.maximum(
        jnp.max(own, axis=0, keepdims=True), jnp.max(other, axis=0, keepdims=True) + offset
    )
    own = jnp.exp(own - top)
    other = jnp.exp(other - (top - offset))
    total = col_sum(own) + col_sum(other)
    inverse = 1.0 / total
    probs = jnp.concatenate([own * inverse, other * inverse], axis=0).astype(BF16)
    return unstack_heads(dot_tn(probs, values)), top + jnp.log(total)


def attend_block_backward(query, keys, values, grad, lse, offset):
    stacked = stack_heads(query * jnp.asarray(HEAD_DIM**-0.5, BF16))
    grads = stack_heads(grad)
    scores = dot_nt(keys, stacked)
    grad_probs = dot_nt(values, grads)
    own = jnp.exp(scores[:IMG] - lse)
    other = jnp.exp(scores[IMG:] - (lse - offset))
    own_t = own * grad_probs[:IMG]
    other_t = other * grad_probs[IMG:]
    delta = col_sum(own_t) + col_sum(other_t)
    grad_scores = jnp.concatenate([own_t - own * delta, other_t - other * delta], axis=0)
    grad_scores = grad_scores.astype(BF16)
    probs = jnp.concatenate([own, other], axis=0).astype(BF16)
    grad_values = dot(probs, grads)
    grad_keys = dot(grad_scores, stacked)
    grad_query = unstack_heads(dot_tn(grad_scores, keys)) * (HEAD_DIM**-0.5)
    return grad_query, grad_keys, grad_values


def forward_kernel(chunk, seg, counts, tokens, vectors, low_qkv, qkv, attended, lse):
    s = pl.program_id(0)
    bias = jnp.concatenate([vectors[2:3, :], jnp.zeros((1, D), F32), vectors[3:4, :]], axis=1)
    for c in range(SEQ // chunk):
        rows = slice(c * chunk, (c + 1) * chunk)
        normed, _, _ = norm_forward(tokens[rows, :].astype(F32), vectors[0:1, :], vectors[1:2, :])
        qkv[rows, :] = (dot(normed.astype(BF16), low_qkv[...]) + bias).astype(BF16)
    linked = links(seg, counts, s)
    for g in range(D // GROUP):
        query_cols, key_cols, value_cols = [
            slice(j * D + g * GROUP, j * D + (g + 1) * GROUP) for j in range(3)
        ]
        out_cols = slice(g * GROUP, (g + 1) * GROUP)
        for b in range(BLOCKS):
            rows = slice(b * IMG, (b + 1) * IMG)
            below, above, with_below, with_above, offset = neighbour(b, linked)
            keys = jnp.concatenate(
                [qkv[rows, key_cols], other_rows(qkv, key_cols, below, above, with_below)], axis=0
            )
            own_values = qkv[rows, value_cols]
            values = jnp.concatenate(
                [own_values, other_rows(qkv, value_cols, below, above, with_below)], axis=0
            )
            mixed, block_lse = attend_block(qkv[rows, query_cols], keys, values, offset)
            mixed = mixed.astype(BF16)
            if b == BLOCKS - 1:
                mixed = jnp.where(b * IMG >= counts[s], own_values, mixed)
            attended[rows, out_cols] = mixed
            lse[g * BLOCKS + b] = block_lse
        attended[BLOCKS * IMG :, out_cols] = qkv[BLOCKS * IMG :, value_cols]


def feed_kernel(
    rows_in,
    chunk,
    counts,
    tokens,
    cotangent,
    attended,
    vectors,
    up_bias,
    low_out,
    low_up,
    low_down,
    layer_out,
    grad_resid,
    grad_attended,
    grad_down,
    grad_up,
    grad_out_w,
    grad_vectors,
    grad_bias,
):
    i = pl.program_id(0)

    @pl.when(i == 0)
    def _():
        for ref in (grad_down, grad_up, grad_out_w, grad_vectors, grad_bias):
            ref[...] = jnp.zeros_like(ref)

    per = SEQ // rows_in
    mixed = attended[...]
    resid = tokens[...].astype(F32) + (dot(mixed, low_out[...]) + vectors[4:5, :])
    normed, hat, spread = norm_forward(resid, vectors[5:6, :], vectors[6:7, :])
    low_two = normed.astype(BF16)
    position = (i % per) * rows_in + lax.broadcasted_iota(jnp.int32, (rows_in, 1), 0)
    grad = jnp.where(position < counts[i // per], cotangent[...].astype(F32), 0.0)
    grad_low = grad.astype(BF16)
    out = jnp.zeros((rows_in, D), F32)
    grad_two = jnp.zeros((rows_in, D), F32)
    for c in range(FF // chunk):
        cols = slice(c * chunk, (c + 1) * chunk)
        hidden = dot(low_two, low_up[:, cols]) + up_bias[:, cols]
        grad_active = dot_nt(grad_low, low_down[cols, :])
        active, slope = gelu_pair(hidden)
        active = active.astype(BF16)
        grad_hidden = grad_active * slope
        grad_hidden_low = grad_hidden.astype(BF16)
        out += dot(active, low_down[cols, :])
        grad_bias[:, cols] += col_sum(grad_hidden)
        grad_down[cols, :] += dot_tn(active, grad_low)
        grad_up[:, cols] += dot_tn(low_two, grad_hidden_low)
        grad_two += dot_nt(grad_hidden_low, low_up[:, cols])
    layer_out[...] = (resid + (out + vectors[7:8, :])).astype(BF16)
    back = grad + norm_backward(grad_two, hat, spread, vectors[5:6, :])
    back_low = back.astype(BF16)
    grad_resid[...] = back
    grad_out_w[...] += dot_tn(mixed, back_low)
    grad_attended[...] = dot_nt(back_low, low_out[...]).astype(BF16)
    grad_vectors[4:5, :] += col_sum(back)
    grad_vectors[5:6, :] += col_sum(grad_two * hat)
    grad_vectors[6:7, :] += col_sum(grad_two)
    grad_vectors[7:8, :] += col_sum(grad)


def backward_kernel(
    chunk,
    seg,
    counts,
    tokens,
    vectors,
    low_qkv,
    qkv,
    grad_attended,
    grad_resid,
    lse,
    token_grad,
    grad_qkv_w,
    grad_vectors,
    grad_qkv,
    key_sum,
    value_sum,
):
    s = pl.program_id(0)

    @pl.when(s == 0)
    def _():
        grad_qkv_w[...] = jnp.zeros_like(grad_qkv_w)
        grad_vectors[...] = jnp.zeros_like(grad_vectors)

    linked = links(seg, counts, s)
    padded = (BLOCKS - 1) * IMG >= counts[s]
    covered = slice(0, BLOCKS * IMG)
    tail = slice(BLOCKS * IMG, SEQ)
    for g in range(D // GROUP):
        query_cols, key_cols, value_cols = [
            slice(j * D + g * GROUP, j * D + (g + 1) * GROUP) for j in range(3)
        ]
        grad_cols = slice(g * GROUP, (g + 1) * GROUP)
        query_bias = jnp.zeros((1, GROUP), F32)
        for b in range(BLOCKS):
            rows = slice(b * IMG, (b + 1) * IMG)
            below, above, with_below, with_above, offset = neighbour(b, linked)
            keys = jnp.concatenate(
                [qkv[rows, key_cols], other_rows(qkv, key_cols, below, above, with_below)], axis=0
            )
            values = jnp.concatenate(
                [qkv[rows, value_cols], other_rows(qkv, value_cols, below, above, with_below)],
                axis=0,
            )
            grad = grad_attended[rows, grad_cols]
            grad_query, grad_keys, grad_values = attend_block_backward(
                qkv[rows, query_cols], keys, values, grad, lse[g * BLOCKS + b], offset
            )
            own_keys, own_values = grad_keys[:IMG], grad_values[:IMG]
            if b == BLOCKS - 1:
                grad_query = jnp.where(padded, 0.0, grad_query)
                own_keys = jnp.where(padded, 0.0, own_keys)
                own_values = jnp.where(padded, grad.astype(F32), own_values)
            query_bias += col_sum(grad_query)
            grad_qkv[rows, query_cols] = grad_query.astype(BF16)
            if b > 0:
                own_keys += jnp.where(with_above, key_sum[rows, :], 0.0)
                own_values += jnp.where(with_above, value_sum[rows, :], 0.0)
            key_sum[rows, :] = own_keys
            value_sum[rows, :] = own_values
            if below is not None:
                key_sum[below, :] = grad_keys[IMG:]
                value_sum[below, :] = grad_values[IMG:]
            if above is not None:
                key_sum[above, :] += jnp.where(with_above, grad_keys[IMG:], 0.0)
                value_sum[above, :] += jnp.where(with_above, grad_values[IMG:], 0.0)
        grad_tail = grad_attended[tail, grad_cols]
        grad_qkv[tail, query_cols] = jnp.zeros_like(grad_tail)
        grad_qkv[tail, key_cols] = jnp.zeros_like(grad_tail)
        grad_qkv[tail, value_cols] = grad_tail
        grad_qkv[covered, key_cols] = key_sum[...].astype(BF16)
        all_values = value_sum[...]
        grad_qkv[covered, value_cols] = all_values.astype(BF16)
        grad_vectors[2:3, grad_cols] += query_bias
        grad_vectors[3:4, grad_cols] += col_sum(all_values) + col_sum(grad_tail.astype(F32))
    for c in range(SEQ // chunk):
        rows = slice(c * chunk, (c + 1) * chunk)
        normed, hat, spread = norm_forward(
            tokens[rows, :].astype(F32), vectors[0:1, :], vectors[1:2, :]
        )
        grad = grad_qkv[rows, :]
        grad_qkv_w[...] += dot_tn(normed.astype(BF16), grad)
        grad_one = dot_nt(grad, low_qkv[...])
        token_grad[rows, :] = grad_resid[rows, :] + norm_backward(
            grad_one, hat, spread, vectors[0:1, :]
        )
        grad_vectors[0:1, :] += col_sum(grad_one * hat)
        grad_vectors[1:2, :] += col_sum(grad_one)


def vmem_params():
    return pltpu.CompilerParams(vmem_limit_bytes=60 * 2**20)


def by_rows(rows, cols):
    return pl.BlockSpec((rows, cols), lambda i: (i, 0))


def whole(*shape):
    return pl.BlockSpec(shape, lambda i: (0,) * len(shape))


def stats_spec():
    return pl.BlockSpec((2 * BLOCKS, 1, PER_GROUP * IMG), lambda i: (i, 0, 0))


def shaped(shape, dtype):
    return jax.ShapeDtypeStruct(shape, dtype)


SCALAR = pl.BlockSpec(memory_space=pltpu.SMEM)


def run_forward(seg, counts, tokens, vectors, low_qkv):
    rows = tokens.shape[0]
    seqs = rows // SEQ
    return pl.pallas_call(
        functools.partial(forward_kernel, 256),
        grid=(seqs,),
        in_specs=[SCALAR, SCALAR, by_rows(SEQ, D), whole(8, D), whole(D, 3 * D)],
        out_specs=[by_rows(SEQ, 3 * D), by_rows(SEQ, D), stats_spec()],
        out_shape=[
            shaped((rows, 3 * D), BF16),
            shaped((rows, D), BF16),
            shaped((seqs * 2 * BLOCKS, 1, PER_GROUP * IMG), F32),
        ],
        compiler_params=vmem_params(),
        name="attend_forward",
    )(seg, counts, tokens, vectors, low_qkv)


def run_feed(counts, tokens, cotangent, attended, vectors, up_bias, low_out, low_up, low_down):
    rows = tokens.shape[0]
    step = 512
    return pl.pallas_call(
        functools.partial(feed_kernel, step, 512),
        grid=(rows // step,),
        in_specs=[
            SCALAR,
            by_rows(step, D),
            by_rows(step, D),
            by_rows(step, D),
            whole(8, D),
            whole(1, FF),
            whole(D, D),
            whole(D, FF),
            whole(FF, D),
        ],
        out_specs=[
            by_rows(step, D),
            by_rows(step, D),
            by_rows(step, D),
            whole(FF, D),
            whole(D, FF),
            whole(D, D),
            whole(8, D),
            whole(1, FF),
        ],
        out_shape=[
            shaped((rows, D), BF16),
            shaped((rows, D), F32),
            shaped((rows, D), BF16),
            shaped((FF, D), F32),
            shaped((D, FF), F32),
            shaped((D, D), F32),
            shaped((8, D), F32),
            shaped((1, FF), F32),
        ],
        compiler_params=vmem_params(),
        name="feed_forward",
    )(counts, tokens, cotangent, attended, vectors, up_bias, low_out, low_up, low_down)


def run_backward(seg, counts, tokens, vectors, low_qkv, qkv, grad_attended, grad_resid, lse):
    rows = tokens.shape[0]
    return pl.pallas_call(
        functools.partial(backward_kernel, 512),
        grid=(rows // SEQ,),
        in_specs=[
            SCALAR,
            SCALAR,
            by_rows(SEQ, D),
            whole(8, D),
            whole(D, 3 * D),
            by_rows(SEQ, 3 * D),
            by_rows(SEQ, D),
            by_rows(SEQ, D),
            stats_spec(),
        ],
        out_specs=[by_rows(SEQ, D), whole(D, 3 * D), whole(8, D)],
        out_shape=[
            shaped((rows, D), F32),
            shaped((D, 3 * D), F32),
            shaped((8, D), F32),
        ],
        scratch_shapes=[
            pltpu.VMEM((SEQ, 3 * D), BF16),
            pltpu.VMEM((BLOCKS * IMG, GROUP), F32),
            pltpu.VMEM((BLOCKS * IMG, GROUP), F32),
        ],
        compiler_params=vmem_params(),
        name="attend_backward",
    )(seg, counts, tokens, vectors, low_qkv, qkv, grad_attended, grad_resid, lse)


def adam_step(weight, moment, square, grad, factor, rate):
    clipped = grad * factor
    moment_new = beta_first * moment + (1.0 - beta_first) * clipped
    square_new = beta_second * square + (1.0 - beta_second) * clipped * clipped
    first_hat = moment_new / (1.0 - beta_first**STEP)
    second_hat = square_new / (1.0 - beta_second**STEP)
    weight_new = weight - rate * (
        first_hat / (jnp.sqrt(second_hat) + adam_eps) + decay_rate * weight
    )
    return (weight_new, moment_new, square_new)


RATES = (
    2.0 / math.sqrt(D),
    8.0 / math.sqrt(D),
    2.0 / math.sqrt(D),
    2.0 / math.sqrt(FF),
    0.5,
    0.5,
)


def body(tokens, cotangent, segment_ids, valid_counts, *state):
    masters, moments, squares = state[:6], state[6:12], state[12:18]
    wide = lax.axis_size("fsdp")
    replicas = lax.axis_size("dp")
    low = [item.astype(BF16) for item in masters]
    full = [
        lax.all_gather(item, "fsdp", axis=1 if k == 4 else 0, tiled=True)
        for k, item in enumerate(low)
    ]
    low_qkv, low_out, low_up, low_down = full[:4]
    vectors = full[4].astype(F32)
    up_bias = full[5].astype(F32).reshape(1, FF)
    qkv, attended, lse = run_forward(segment_ids, valid_counts, tokens, vectors, low_qkv)
    (
        layer_out,
        grad_resid,
        grad_attended,
        grad_down,
        grad_up,
        grad_out_w,
        late_vectors,
        grad_bias,
    ) = run_feed(
        valid_counts, tokens, cotangent, attended, vectors, up_bias, low_out, low_up, low_down
    )
    token_grad, grad_qkv_w, early_vectors = run_backward(
        segment_ids,
        valid_counts,
        tokens,
        vectors,
        low_qkv,
        qkv,
        grad_attended,
        grad_resid,
        lse,
    )
    partial = (
        grad_qkv_w,
        grad_out_w,
        grad_up,
        grad_down,
        early_vectors + late_vectors,
        grad_bias.reshape(FF),
    )
    grads = []
    for k, item in enumerate(partial):
        shard = lax.psum_scatter(item, "fsdp", scatter_dimension=1 if k == 4 else 0, tiled=True)
        grads.append(lax.psum(shard.astype(BF16), "dp").astype(F32))
    local_total = jnp.sum(grads[0] * grads[0])
    for item in grads[1:]:
        local_total = local_total + jnp.sum(item * item)
    grad_norm = jnp.sqrt(lax.psum(local_total, "fsdp"))
    bound = 0.005 * math.sqrt(tokens.shape[0] * wide * replicas * PARAMS)
    factor = jnp.minimum(1.0, bound / grad_norm)
    fresh = [
        adam_step(masters[k], moments[k], squares[k], grads[k], factor, RATES[k]) for k in range(6)
    ]
    return (
        layer_out,
        token_grad,
        grad_norm,
        *(item[0] for item in fresh),
        *(item[1] for item in fresh),
        *(item[2] for item in fresh),
    )


def solution(mesh):
    rows = P(("fsdp", "dp"), None)
    state = (
        P("fsdp", None),
        P("fsdp", None),
        P("fsdp", None),
        P("fsdp", None),
        P(None, "fsdp"),
        P("fsdp"),
    )
    return jax.shard_map(
        body,
        mesh=mesh,
        in_specs=(rows, rows, rows, P(("fsdp", "dp")), *state, *state, *state),
        out_specs=(rows, rows, P(), *state, *state, *state),
        check_vma=False,
    )
```

time: 1220 us -> 843 us (0.69); the launches traced: 1200 us -> 842 us
  matrix products: 252 us -> 0 us
  local copies, waits for them, and re-layouts: 204 us -> 3.11 us
  waiting for transfers between devices: 385 us -> 489 us
  other arithmetic: 125 us -> 26.4 us
  Pallas kernels: 0 us -> 93 us
    dot_general x40 -> x0, matrix products: 252 us -> none  [the longest x8 58.7 us: one_block(): jnp.einsum('qhd,khd->hqk', q_rows, keys, preferred_element_type=jnp.float32)]
    dynamic_update_slice x24 -> x0, local copies, waits for them, and re-layouts: 116 us -> none  [the longest x8 82.2 us: attend_backward(): lax.scan(one_block, (zeros, zeros), (jnp.arange(length // block, dtype=jn...]
    pallas_call x0 -> x3, Pallas kernels: none -> 93 us  [the longest x1 41.9 us: run_feed(): pl.pallas_call(functools.partial(feed_kernel, step, 512), grid=(rows // s...]
    all_gather x3, waiting for transfers between devices: 0.04 us -> 43.9 us  [body(): lax.all_gather(item, 'fsdp', axis=1 if k == 4 else 0, tiled=True)]
    convert_element_type x13 -> x8, other arithmetic: 49.2 us -> 11.3 us  [the longest x4 5.67 us: body(): low = [item.astype(BF16) for item in masters]]
    reduce_sum x11 -> x0, other arithmetic: 34.8 us -> none  [the longest x4 17 us: one_block(): total = jnp.sum(expo, axis=-1, keepdims=True)]
    unnamed x10, waiting for transfers between devices: 0.15 us -> 33.4 us
    reduce_scatter x4, waiting for transfers between devices: 370 us -> 397 us  [body(): lax.psum_scatter(item, 'fsdp', scatter_dimension=1 if k == 4 else 0, tile...]
  transfers between devices with their start and end apart: 9 -> 9, of which waited for: 5 -> 7; matrix products, arithmetic and copies ran while one was open for 16% -> 2% of each run, Pallas kernels for 0% -> 2%
where the time goes in v1:
time: 843 us; the launch traced here: 842 us
  waiting for transfers between devices  489 us (58%)
  blocking collectives  209 us (25%)
  Pallas kernels  93 us (11%)
  other arithmetic  26.4 us (3%)
  between operations  20.5 us (2%)
    reduce_scatter x4, waiting for transfers between devices, body(): lax.psum_scatter(item, 'fsdp', scatter_dimension=1 if k == 4 else 0, tile...  397 us
    all_gather x3, blocking collectives, body(): lax.all_gather(item, 'fsdp', axis=1 if k == 4 else 0, tiled=True)  123 us
    all_gather x3, waiting for transfers between devices, body(): lax.all_gather(item, 'fsdp', axis=1 if k == 4 else 0, tiled=True)  43.9 us
    psum x1, blocking collectives, body(): grad_norm = jnp.sqrt(lax.psum(local_total, 'fsdp'))  42.5 us
    pallas_call x1, Pallas kernels, run_feed(): pl.pallas_call(functools.partial(feed_kernel, step, 512), grid=(rows // s...  41.9 us
    unnamed x1, blocking collectives  39.9 us
    pallas_call x1, Pallas kernels, run_backward(): pl.pallas_call(functools.partial(backward_kernel, 512), grid=(rows // SEQ...  33.9 us
    unnamed x10, waiting for transfers between devices  33.4 us
  transfers between devices with their start and end apart: 9, of which 7 were waited for; matrix products, arithmetic and copies ran while one was open for 2% of the time, Pallas kernels for 2%

profile of v1, /device:TPU:0, one launch (start us, length us, event | category | flops | bytes accessed | tf_op | source)
XLA Modules:
  0.0 841.8 jit_solution(1694748296518011879)
XLA Ops:
  7.2 1.6 convert_element_type.60
  8.9 1.6 convert_element_type.64
  10.6 1.6 convert_element_type.63
  13.0 42.5 %all-gather = bf16[16,32,8]{1,2,0:T(8,128)(2,1)S(1)} all-gather(bf16[1,32,8]{1,2,0:T(8,128)(2,1)S(1)} %convert_bitcast_fusion), channel_id=1, replica_groups=mesh['fsdp'=16,'dp'=2] {'fsdp'}, dimensions={0}, use_global_device_ids=true | all-gather | bytes 8704 | tf_op jit(solution)/shard_map/all_gather | solution.py:478
  56.2 0.8 convert_element_type.62
  57.7 35.3 %all-gather.1 = bf16[16,1,128]{2,1,0:T(2,128)(2,1)S(1)} all-gather(bf16[1,1,128]{2,1,0:T(2,128)(2,1)S(1)} %convert_bitcast_fusion.1), channel_id=1, replica_groups=mesh['fsdp'=16,'dp'=2] {'fsdp'}, dimensions={0}, use_global_device_ids=true | all-gather | bytes 4352 | tf_op jit(solution)/shard_map/all_gather | solution.py:478
  93.0 45.5 %all_gather.21.low_out = bf16[512,512]{1,0:T(8,128)(2,1)} all-gather(bf16[32,512]{1,0:T(8,128)(2,1)S(1)} %convert_element_type.62), channel_id=1, replica_groups=mesh['fsdp'=16,'dp'=2] {'fsdp'}, dimensions={0}, use_global_device_ids=true | all-gather | bytes 557056 | tf_op jit(solution)/shard_map/all_gather | solution.py:478
  139.2 17.2 %attend_forward.1 = (bf16[2048,1536]{1,0:T(8,128)(2,1)}, bf16[2048,512]{1,0:T(8,128)(2,1)}, f32[20,1,768]{2,1,0:T(1,128)}) custom-call(s32[2,1024]{1,0:T(2,128)} %seg.3, s32[2]{0:T(128)} %counts.5, bf16[2048,512]{1,0:T(8,128)(2,1)} %tokens.5, f32[8,512]{1,0:T(8,128)} %bitcast.17, bf16[512,1536]{1,0:T(8,128)(2,1)} %all-gather.6.cloned.1.call-done.low_qkv), custom_call_target="tpu_custom_call" | custom-call | tf_op jit(solution)/shard_map/attend_forward/pallas_call | solution.py:361
  156.4 43.9 %all-gather.8.cloned.1.call-done.low_up = bf16[512,2048]{1,0:T(8,128)(2,1)} async-done(((bf16[32,2048]{1,0:T(8,128)(2,1)}), bf16[512,2048]{1,0:T(8,128)(2,1)}) %all-gather.8.cloned.1.call-update) | async-done | bytes 2097168 | tf_op jit(solution)/shard_map/all_gather | solution.py:478
  200.2 41.9 %feed_forward.1 = (bf16[2048,512]{1,0:T(8,128)(2,1)}, f32[2048,512]{1,0:T(8,128)}, bf16[2048,512]{1,0:T(8,128)(2,1)}, f32[2048,512]{1,0:T(8,128)}, f32[512,2048]...) custom-call(s32[2]{0:T(128)} %counts.5, bf16[2048,512]{1,0:T(8,128)(2,1)} %tokens.5, ...), custom_call_target="tpu_custom_call" | custom-call | tf_op jit(solution)/shard_map/feed_forward/pallas_call | solution.py:379
  242.1 33.9 %attend_backward.1 = (f32[2048,512]{1,0:T(8,128)}, f32[512,1536]{1,0:T(8,128)}, f32[8,512]{1,0:T(8,128)}) custom-call(s32[2,1024]{1,0:T(2,128)} %seg.3, s32[2]{0:T(128)} %counts.5, bf16[2048,512]{1,0:T(8,128)(2,1)} %tokens.5, f32[8,512]{1,0:T(8,128)} %bitcast.19, bf16[512,1536]{1,0:T(8,128)(2,1)} %all-gather.6.cloned.1.call-done.low_qkv, ...), custom_call_target="tpu_custom_call" | custom-call | tf_op jit(solution)/shard_map/attend_backward/pallas_call | solution.py:420
  276.8 0.8 copy.45
  281.7 39.9 %all-reduce = bf16[2048]{0:T(1024)(128)(2,1)S(1)} all-reduce(f32[2048]{0:T(1024)S(1)} %bitcast.21), channel_id=7, replica_groups=mesh['fsdp'=16,'dp'=2] {'fsdp'}, use_global_device_ids=true, to_apply=%region_15.0.clone | all-reduce | flops 2048 | bytes 12288
  321.8 30.9 %reduce-scatter.16.cloned.1.call-done = f32[32,8]{1,0:T(8,128)} async-done(((f32[512,8]{1,0:T(8,128)}), f32[32,8]{1,0:T(8,128)}) %reduce-scatter.16.cloned.1.call-update) | async-done | bytes 1040
  352.7 0.8 copy.46
  353.5 75.4 %reduce-scatter.10.cloned.1.call-done = f32[32,512]{1,0:T(8,128)} async-done(((f32[512,512]{1,0:T(8,128)}), f32[32,512]{1,0:T(8,128)}) %reduce-scatter.10.cloned.1.call-update) | async-done | bytes 65552 | tf_op jit(solution)/shard_map/reduce_scatter | solution.py:518
  428.9 0.8 convert_element_type.67
  429.8 130.9 %reduce-scatter.8.cloned.1.call-done = f32[32,1536]{1,0:T(8,128)} async-done(((f32[512,1536]{1,0:T(8,128)}), f32[32,1536]{1,0:T(8,128)}) %reduce-scatter.8.cloned.1.call-update) | async-done | bytes 196624 | tf_op jit(solution)/shard_map/reduce_scatter | solution.py:518
  560.7 1.6 convert_element_type.65
  562.3 95.2 %reduce-scatter.12.cloned.1.call-done = f32[32,2048]{1,0:T(8,128)} async-done(((f32[512,2048]{1,0:T(8,128)}), f32[32,2048]{1,0:T(8,128)}) %reduce-scatter.12.cloned.1.call-update) | async-done | bytes 262160 | tf_op jit(solution)/shard_map/reduce_scatter | solution.py:518
  657.4 1.6 convert_element_type.69
  659.0 95.4 %reduce-scatter.14.cloned.1.call-done = f32[128,512]{1,0:T(8,128)} async-done(((f32[2048,512]{1,0:T(8,128)}), f32[128,512]{1,0:T(8,128)}) %reduce-scatter.14.cloned.1.call-update) | async-done | bytes 262160 | tf_op jit(solution)/shard_map/reduce_scatter | solution.py:518
  754.5 1.6 convert_element_type.71
  756.1 3.6 all-reduce.1
  761.5 14.8 %all-reduce.5.cloned.1.call-done = (bf16[32,1536]{1,0:T(8,128)(2,1)}, bf16[32,2048]{1,0:T(8,128)(2,1)}, bf16[128,512]{1,0:T(8,128)(2,1)}) async-done(((bf16[32,1536]{1,0:T(8,128)(2,1)}, bf16[32,2048]{1,0:T(8,128)(2,1)}, bf16[128,512]{1,0:T(8,128)(2,1)}), (bf16[32,1536]{1,0:T(8,128)(2,1)}, bf16[32,2048]{1,0:T(8,128)(2,1)}, bf16[128,512]{1,0:T(8,128)(2,1)})) %all-reduce.5.cloned.1.call-update) | async-done | bytes 360464 | tf_op jit(solution)/shard_map/psum | solution.py:519
  776.3 1.6 fusion.4
  777.9 1.6 fusion
  779.6 1.6 fusion.1
  785.0 42.5 %psum.55 = f32[]{:T(128)} all-reduce(f32[]{:T(128)S(6)} %add.139), channel_id=1, replica_groups=mesh['fsdp'=16,'dp'=2] {'fsdp'}, use_global_device_ids=true, to_apply=%region_18.0 | all-reduce | flops 1 | bytes 8 | tf_op jit(solution)/shard_map/psum | solution.py:523
  829.5 1.9 multiply_subtract_fusion
  831.5 1.0 multiply_subtract_fusion.1
  833.2 0.9 multiply_subtract_fusion.2
  (80 shorter events, 10.6 us)
Async XLA Ops:
  7.2 132.0 %all-gather.6.cloned.1.call-start = ((), (), s32[]{:S(2)}) async-start(), calls=%async_computation.5 | async-start | bytes 1671168 | tf_op jit(solution)/shard_map/all_gather | solution.py:478
  8.8 147.5 %all-gather.10.cloned.1.call-start = ((), (), s32[]{:S(2)}) async-start(), calls=%async_computation.7 | async-start | bytes 2228224 | tf_op jit(solution)/shard_map/all_gather | solution.py:478
  10.5 189.7 %all-gather.8.cloned.1.call-start = ((), (), s32[]{:S(2)}) async-start(), calls=%async_computation.6 | async-start | bytes 2228224 | tf_op jit(solution)/shard_map/all_gather | solution.py:478
  12.2 340.4 %reduce-scatter.16.cloned.1.call-start = ((), (), s32[]{:S(2)}) async-start(), calls=%async_computation.12 | async-start | bytes 278528
  242.1 34.0 %copy-start.14 = (f32[8,512]{1,0:T(8,128)S(1)}, f32[8,512]{1,0:T(8,128)}, u32[]{:S(2)}) copy-start(f32[8,512]{1,0:T(8,128)} %get-tuple-element.47) | copy-start | bytes 49156
  277.7 151.2 %reduce-scatter.10.cloned.1.call-start = ((), (), s32[]{:S(2)}) async-start(), calls=%async_computation.9 | async-start | bytes 1114112 | tf_op jit(solution)/shard_map/reduce_scatter | solution.py:518
  278.3 282.4 %reduce-scatter.8.cloned.1.call-start = ((), (), s32[]{:S(2)}) async-start(), calls=%async_computation.8 | async-start | bytes 3342336 | tf_op jit(solution)/shard_map/reduce_scatter | solution.py:518
  278.8 378.6 %reduce-scatter.12.cloned.1.call-start = ((), (), s32[]{:S(2)}) async-start(), calls=%async_computation.10 | async-start | bytes 4456448 | tf_op jit(solution)/shard_map/reduce_scatter | solution.py:518
  279.6 474.9 %reduce-scatter.14.cloned.1.call-start = ((), (), s32[]{:S(2)}) async-start(), calls=%async_computation.11 | async-start | bytes 4456448 | tf_op jit(solution)/shard_map/reduce_scatter | solution.py:518
  279.6 0.8 copy-start.22
  279.7 2.1 copy-start.16
  279.7 548.6 %copy-start.19 = (f32[128]{0:T(128)S(1)}, f32[128]{0:T(128)}, u32[]{:S(2)}) copy-start(f32[128]{0:T(128)} %param.31) | copy-start | bytes 1540
  279.7 548.6 %copy-start.20 = (f32[128]{0:T(128)S(1)}, f32[128]{0:T(128)}, u32[]{:S(2)}) copy-start(f32[128]{0:T(128)} %param.37) | copy-start | bytes 1540
  279.7 548.6 %copy-start.21 = (f32[128]{0:T(128)S(1)}, f32[128]{0:T(128)}, u32[]{:S(2)}) copy-start(f32[128]{0:T(128)} %param.43) | copy-start | bytes 1540
  279.7 549.2 %copy-start.15 = (f32[8,32]{1,0:T(8,128)S(1)}, f32[8,32]{1,0:T(8,128)}, u32[]{:S(2)}) copy-start(f32[8,32]{1,0:T(8,128)} %param.30) | copy-start | bytes 3076
  279.7 549.2 %copy-start.17 = (f32[8,32]{1,0:T(8,128)S(1)}, f32[8,32]{1,0:T(8,128)}, u32[]{:S(2)}) copy-start(f32[8,32]{1,0:T(8,128)} %param.36) | copy-start | bytes 3076
  279.7 549.1 %copy-start.18 = (f32[8,32]{1,0:T(8,128)S(1)}, f32[8,32]{1,0:T(8,128)}, u32[]{:S(2)}) copy-start(f32[8,32]{1,0:T(8,128)} %param.42) | copy-start | bytes 3076
  280.3 549.2 %copy-start = (f32[128,512]{1,0:T(8,128)S(1)}, f32[128,512]{1,0:T(8,128)}, u32[]{:S(2)}) copy-start(f32[128,512]{1,0:T(8,128)} %param.29) | copy-start | bytes 786436
  280.4 549.1 %copy-start.5 = (f32[128,512]{1,0:T(8,128)S(1)}, f32[128,512]{1,0:T(8,128)}, u32[]{:S(2)}) copy-start(f32[128,512]{1,0:T(8,128)} %param.35) | copy-start | bytes 786436
  280.4 549.1 %copy-start.6 = (f32[128,512]{1,0:T(8,128)S(1)}, f32[128,512]{1,0:T(8,128)}, u32[]{:S(2)}) copy-start(f32[128,512]{1,0:T(8,128)} %param.41) | copy-start | bytes 786436
  280.4 551.1 %copy-start.1 = (f32[32,2048]{1,0:T(8,128)S(1)}, f32[32,2048]{1,0:T(8,128)}, u32[]{:S(2)}) copy-start(f32[32,2048]{1,0:T(8,128)} %param.28) | copy-start | bytes 786436
  280.4 551.0 %copy-start.7 = (f32[32,2048]{1,0:T(8,128)S(1)}, f32[32,2048]{1,0:T(8,128)}, u32[]{:S(2)}) copy-start(f32[32,2048]{1,0:T(8,128)} %param.34) | copy-start | bytes 786436
  280.4 551.0 %copy-start.8 = (f32[32,2048]{1,0:T(8,128)S(1)}, f32[32,2048]{1,0:T(8,128)}, u32[]{:S(2)}) copy-start(f32[32,2048]{1,0:T(8,128)} %param.40) | copy-start | bytes 786436
  280.4 495.9 %all-reduce.5.cloned.1.call-start = ((), (), s32[]{:S(2)}) async-start(), calls=%async_computation.13 | async-start | bytes 720896 | tf_op jit(solution)/shard_map/psum | solution.py:519
  756.1 76.4 %copy-start.9 = (f32[32,512]{1,0:T(8,128)S(1)}, f32[32,512]{1,0:T(8,128)}, u32[]{:S(2)}) copy-start(f32[32,512]{1,0:T(8,128)} %param.27) | copy-start | bytes 196612
  756.1 76.4 %copy-start.12 = (f32[32,512]{1,0:T(8,128)S(1)}, f32[32,512]{1,0:T(8,128)}, u32[]{:S(2)}) copy-start(f32[32,512]{1,0:T(8,128)} %param.33) | copy-start | bytes 196612
  756.1 76.4 %copy-start.13 = (f32[32,512]{1,0:T(8,128)S(1)}, f32[32,512]{1,0:T(8,128)}, u32[]{:S(2)}) copy-start(f32[32,512]{1,0:T(8,128)} %param.39) | copy-start | bytes 196612
  776.3 55.1 %copy-start.3 = (bf16[32,2048]{1,0:T(8,128)(2,1)S(1)}, bf16[32,2048]{1,0:T(8,128)(2,1)}, u32[]{:S(2)}) copy-start(bf16[32,2048]{1,0:T(8,128)(2,1)} %get-tuple-element.53) | copy-start | bytes 393220
  777.9 55.3 %copy-start.2 = (f32[32,1536]{1,0:T(8,128)S(1)}, f32[32,1536]{1,0:T(8,128)}, u32[]{:S(2)}) copy-start(f32[32,1536]{1,0:T(8,128)} %param.26) | copy-start | bytes 589828
  777.9 55.3 %copy-start.4 = (bf16[32,1536]{1,0:T(8,128)(2,1)S(1)}, bf16[32,1536]{1,0:T(8,128)(2,1)}, u32[]{:S(2)}) copy-start(bf16[32,1536]{1,0:T(8,128)(2,1)} %get-tuple-element.52) | copy-start | bytes 294916
  777.9 55.3 %copy-start.10 = (f32[32,1536]{1,0:T(8,128)S(1)}, f32[32,1536]{1,0:T(8,128)}, u32[]{:S(2)}) copy-start(f32[32,1536]{1,0:T(8,128)} %param.32) | copy-start | bytes 589828
  777.9 55.3 %copy-start.11 = (f32[32,1536]{1,0:T(8,128)S(1)}, f32[32,1536]{1,0:T(8,128)}, u32[]{:S(2)}) copy-start(f32[32,1536]{1,0:T(8,128)} %param.38) | copy-start | bytes 589828
Sparse Core Ops, SparseCore 0:
  11.4 60.5 all-gather.5
  75.3 61.2 all-gather.9
  140.0 60.1 all-gather.7
  277.8 74.8 reduce-scatter.15
  354.9 73.9 reduce-scatter.9
  433.7 126.8 reduce-scatter.7
  563.0 94.3 reduce-scatter.11
  659.7 94.7 reduce-scatter.13
  758.1 18.1 all-reduce.4

commit v2 on v1

--- a/solution.py
+++ b/solution.py
@@ -469,18 +469,383 @@
 )
 
 
-def body(tokens, cotangent, segment_ids, valid_counts, *state):
-    masters, moments, squares = state[:6], state[6:12], state[12:18]
-    wide = lax.axis_size("fsdp")
-    replicas = lax.axis_size("dp")
-    low = [item.astype(BF16) for item in masters]
-    full = [
-        lax.all_gather(item, "fsdp", axis=1 if k == 4 else 0, tiled=True)
-        for k, item in enumerate(low)
+MESH = pl.DeviceIdType.MESH
+COLS = 4
+
+
+class Place:
+    def __init__(self, planes):
+        self.planes = planes
+        self.i = lax.axis_index("fsdp")
+        self.c = c = lax.axis_index("dp")
+        self.q = q = lax.rem(self.i, COLS)
+        self.z = self.i // COLS
+        x, y = lax.rem(q, 2), q // 2
+        self.qx = y * 2 + (1 - x)
+        self.qy = (1 - y) * 2 + x
+        self.qa = c * self.qx + (1 - c) * self.qy
+        self.qb = c * self.qy + (1 - c) * self.qx
+        self.qd = COLS - 1 - q
+        self.at_a = (self.z * COLS + self.qa, c)
+        self.at_b = (self.z * COLS + self.qb, c)
+        self.at_x = (self.z * COLS + self.qx, c)
+        self.at_y = (self.z * COLS + self.qy, c)
+        self.partner = (self.i, 1 - c)
+
+    def plane(self, step):
+        return lax.rem(self.z + step, self.planes)
+
+    def along(self, step):
+        return (self.plane(step) * COLS + self.q, self.c)
+
+    def greet(self):
+        barrier = pltpu.get_barrier_semaphore()
+        friends = [self.along(step) for step in range(1, self.planes)]
+        friends += [self.at_a, self.at_b, self.partner]
+        for device in friends:
+            pl.semaphore_signal(barrier, inc=1, device_id=device, device_id_type=MESH)
+        pl.semaphore_wait(barrier, len(friends))
+
+
+def remote(source, target, send, recv, device):
+    return pltpu.make_async_remote_copy(
+        src_ref=source,
+        dst_ref=target,
+        send_sem=send,
+        recv_sem=recv,
+        device_id=device,
+        device_id_type=MESH,
+    )
+
+
+class Gather:
+    def __init__(self, place, full, send, recv):
+        self.full, self.place = full, place
+        p, c = place, place.c
+        self.first = [
+            remote(full.at[p.z, p.q, c], full.at[p.z, p.q, c], send.at[k], recv.at[k], p.along(k + 1))
+            for k in range(p.planes - 1)
+        ]
+        base = p.planes - 1
+        moves = [
+            (p.q, p.at_a),
+            (p.q, p.at_b),
+            (p.qa, p.at_b),
+            (p.q, p.partner),
+            (p.qa, p.partner),
+            (p.qb, p.partner),
+            (p.qd, p.partner),
+        ]
+        self.moves = [
+            remote(full.at[:, col, c], full.at[:, col, c], send.at[base + k], recv.at[base + k], device)
+            for k, (col, device) in enumerate(moves)
+        ]
+
+    @staticmethod
+    def count(planes):
+        return planes + 6
+
+    def begin(self):
+        for copy in self.first:
+            copy.start()
+
+    def spread(self):
+        for copy in self.first:
+            copy.wait_recv()
+        for k in (0, 1, 3):
+            self.moves[k].start()
+
+    def forward(self):
+        self.moves[0].wait_recv()
+        self.moves[2].start()
+        self.moves[4].start()
+        self.moves[1].wait_recv()
+        self.moves[5].start()
+
+    def last(self):
+        self.moves[2].wait_recv()
+        self.moves[6].start()
+
+    def arrive(self):
+        for k in range(3, 7):
+            self.moves[k].wait_recv()
+
+    def drain(self):
+        for copy in (*self.first, *self.moves):
+            copy.wait_send()
+
+
+class Scatter:
+    def __init__(self, place, total, bufs, result, send, recv):
+        self.place, self.total, self.result = place, total, result
+        self.out_c, self.in_c, self.out_b, self.in_b = bufs[:4]
+        self.out_a, self.in_a, self.out_z, self.in_z = bufs[4:]
+        p = place
+        self.order = (p.qa, p.qd, p.qb, p.q)
+        self.to_core = [
+            remote(self.out_c.at[k], self.in_c.at[k], send.at[k], recv.at[k], p.partner)
+            for k in range(4)
+        ]
+        self.to_b = [
+            remote(self.out_b.at[k], self.in_b.at[k], send.at[4 + k], recv.at[4 + k], p.at_b)
+            for k in range(2)
+        ]
+        self.to_a = remote(self.out_a, self.in_a, send.at[6], recv.at[6], p.at_a)
+        self.to_z = [
+            remote(self.out_z.at[k], self.in_z.at[k], send.at[7 + k], recv.at[7 + k], p.along(k + 1))
+            for k in range(p.planes - 1)
+        ]
+        n = 6 + p.planes
+        half = result.at[p.c]
+        self.to_both = remote(half, half, send.at[n], recv.at[n], p.partner)
+
+    @staticmethod
+    def count(planes):
+        return planes + 7
+
+    @staticmethod
+    def buffers(planes, rows, cols):
+        shapes = [(4, planes)] * 2 + [(2, planes)] * 2 + [(planes,)] * 2 + [(planes - 1,)] * 2
+        return [pltpu.VMEM((*shape, rows, cols), BF16) for shape in shapes]
+
+    def begin(self):
+        for k in range(4):
+            self.out_c[k] = self.total[:, self.order[k], 1 - self.place.c].astype(BF16)
+            self.to_core[k].start()
+
+    def second(self):
+        p = self.place
+        for k, col in ((1, p.qd), (0, p.qb)):
+            self.to_core[k].wait_recv()
+            mine = self.total[:, col, p.c] + self.in_c[k].astype(F32)
+            self.out_b[k] = mine.astype(BF16)
+            self.to_b[k].start()
+
+    def first(self):
+        p = self.place
+        self.to_core[2].wait_recv()
+        self.to_b[1].wait_recv()
+        mine = self.total[:, p.qa, p.c] + self.in_c[2].astype(F32) + self.in_b[1].astype(F32)
+        self.out_a[...] = mine.astype(BF16)
+        self.to_a.start()
+
+    def planes(self):
+        p = self.place
+        self.to_core[3].wait_recv()
+        self.to_b[0].wait_recv()
+        self.to_a.wait_recv()
+
+        def mine(z):
+            local = self.total[z, p.q, p.c] + self.in_c[3, z].astype(F32)
+            return local + self.in_b[0, z].astype(F32) + self.in_a[z].astype(F32)
+
+        for k in range(p.planes - 1):
+            self.out_z[k] = mine(p.plane(k + 1)).astype(BF16)
+            self.to_z[k].start()
+        self.result[p.c] = mine(p.z)
+
+    def finish(self):
+        p = self.place
+        for copy in self.to_z:
+            copy.wait_recv()
+        shard = self.result[p.c]
+        for k in range(p.planes - 1):
+            shard = shard + self.in_z[k].astype(F32)
+        self.result[p.c] = shard
+        self.to_both.start()
+        square = shard * shard
+        lanes = sum(square[:, k : k + 128] for k in range(0, square.shape[1], 128))
+        return jnp.sum(lanes.reshape(-1, 8, 128), axis=0)
+
+    def drain(self):
+        self.to_both.wait_recv()
+        for copy in (*self.to_core, *self.to_b, self.to_a, *self.to_z, self.to_both):
+            copy.wait_send()
+
+
+def sum_over_all(place, part, out, slots, send, recv):
+    p = place
+    out[0] = part
+    slots[p.z] = part
+    copies = [
+        remote(out.at[0], slots.at[p.z], send.at[k], recv.at[k], p.along(k + 1))
+        for k in range(p.planes - 1)
     ]
-    low_qkv, low_out, low_up, low_down = full[:4]
-    vectors = full[4].astype(F32)
-    up_bias = full[5].astype(F32).reshape(1, FF)
+    for copy in copies:
+        copy.start()
+    for copy in copies:
+        copy.wait_recv()
+    total = slots[0]
+    for k in range(1, p.planes):
+        total = total + slots[k]
+    for k, device in enumerate((p.at_x, p.at_y, p.partner)):
+        out[1 + k] = total
+        n = p.planes - 1 + k
+        copy = remote(out.at[1 + k], slots.at[n + 1], send.at[n], recv.at[n], device)
+        copy.start()
+        copy.wait_recv()
+        copies.append(copy)
+        total = total + slots[n + 1]
+    for copy in copies:
+        copy.wait_send()
+    return total
+
+
+def small_shard(place, vectors, up_bias):
+    def tile(rows):
+        for axis, full in ((1, 128), (0, 8)):
+            short = list(rows.shape)
+            short[axis] = full - short[axis]
+            if short[axis]:
+                rows = jnp.concatenate([rows, jnp.zeros(short, F32)], axis=axis)
+        return rows
+
+    rows, bias = tile(vectors[...]), tile(up_bias[...])
+    half = jnp.where(place.c == 0, rows, bias)
+    return jnp.concatenate([half, jnp.zeros((8, 128), F32)], axis=0).astype(BF16)
+
+
+def gather_kernel(planes, *refs):
+    shards, vectors, up_bias = refs[:4], refs[4], refs[5]
+    full, all_vectors, all_bias = refs[6:10], refs[10], refs[11]
+    small, send, recv = refs[12:]
+    p = Place(planes)
+    per, long = vectors.shape[1], up_bias.shape[1]
+    small[p.z, p.q, p.c] = small_shard(p, vectors, up_bias)
+    for shard, target in zip(shards, full):
+        target[p.z, p.q, p.c] = shard[p.c].astype(BF16)
+    p.greet()
+    gathers = [
+        Gather(p, ref, send.at[k], recv.at[k]) for k, ref in enumerate((small, *full))
+    ]
+    for stage in (Gather.begin, Gather.spread, Gather.forward, Gather.last, Gather.arrive):
+        for item in gathers:
+            stage(item)
+    for s in range(planes * COLS):
+        rows = small[s // COLS, s % COLS, 0].astype(F32)
+        bias = small[s // COLS, s % COLS, 1].astype(F32)
+        all_vectors[:, s * per : (s + 1) * per] = rows[:8, :per]
+        all_bias[:, s * long : (s + 1) * long] = bias[:1, :long]
+    for item in gathers:
+        item.drain()
+
+
+def run_gather(planes, masters):
+    shards = [item.reshape(2, item.shape[0] // 2, item.shape[1]) for item in masters[:4]]
+    vmem = pl.BlockSpec(memory_space=pltpu.VMEM)
+    sems = pltpu.SemaphoreType.DMA((5, Gather.count(planes)))
+    full = pl.pallas_call(
+        functools.partial(gather_kernel, planes),
+        in_specs=[vmem] * 6,
+        out_specs=[vmem] * 6,
+        out_shape=[shaped((planes, COLS, *item.shape), BF16) for item in shards]
+        + [shaped((8, D), F32), shaped((1, FF), F32)],
+        scratch_shapes=[pltpu.VMEM((planes, COLS, 2, 16, 128), BF16), sems, sems],
+        compiler_params=pltpu.CompilerParams(
+            vmem_limit_bytes=60 * 2**20, collective_id=1, has_side_effects=True
+        ),
+        name="gather_weights",
+    )(*shards, masters[4], masters[5].reshape(1, -1))
+    return [item.reshape(-1, item.shape[-1]) for item in full[:4]] + list(full[4:])
+
+
+def scatter_kernel(planes, per, long, *refs):
+    totals, early, late, bias = refs[:4], refs[4], refs[5], refs[6]
+    results, norm, rest = refs[7:12], refs[12], refs[13:]
+    small, rest = rest[0], rest[1:]
+    bufs, (send, recv, out, slots, norm_send, norm_recv) = rest[:40], rest[40:]
+    p = Place(planes)
+    small[...] = jnp.zeros_like(small)
+    for s in range(planes * COLS):
+        cols = slice(s * per, (s + 1) * per)
+        small[s // COLS, s % COLS, 0, 0:8, 0:per] = early[:, cols] + late[:, cols]
+        small[s // COLS, s % COLS, 1, 0:1, 0:long] = bias[:, s * long : (s + 1) * long]
+    scatters = [
+        Scatter(p, total, bufs[8 * k : 8 * k + 8], results[k], send.at[k], recv.at[k])
+        for k, total in enumerate((*totals, small))
+    ]
+    p.greet()
+    for stage in (Scatter.begin, Scatter.second, Scatter.first, Scatter.planes):
+        for item in scatters:
+            stage(item)
+    part = scatters[0].finish()
+    for item in scatters[1:]:
+        part = part + item.finish()
+    norm[...] = sum_over_all(p, part, out, slots, norm_send, norm_recv)
+    for item in scatters:
+        item.drain()
+
+
+def run_scatter(planes, per, long, totals, early, late, bias):
+    halves = [
+        item.reshape(planes, COLS, 2, item.shape[0] // (planes * COLS * 2), item.shape[1])
+        for item in totals
+    ]
+    shapes = [item.shape[3:] for item in halves] + [(16, 128)]
+    vmem = pl.BlockSpec(memory_space=pltpu.VMEM)
+    sems = pltpu.SemaphoreType.DMA((5, Scatter.count(planes)))
+    norm_sems = pltpu.SemaphoreType.DMA((planes + 2,))
+    scratch = [pltpu.VMEM((planes, COLS, 2, 16, 128), F32)]
+    for shape in shapes:
+        scratch += Scatter.buffers(planes, *shape)
+    scratch += [sems, sems]
+    scratch += [pltpu.VMEM((4, 8, 128), F32), pltpu.VMEM((planes + 3, 8, 128), F32)]
+    scratch += [norm_sems, norm_sems]
+    return pl.pallas_call(
+        functools.partial(scatter_kernel, planes, per, long),
+        in_specs=[vmem] * 7,
+        out_specs=[vmem] * 6,
+        out_shape=[shaped((2, *shape), F32) for shape in shapes] + [shaped((8, 128), F32)],
+        scratch_shapes=scratch,
+        compiler_params=pltpu.CompilerParams(
+            vmem_limit_bytes=62 * 2**20, collective_id=2, has_side_effects=True
+        ),
+        name="scatter_gradients",
+    )(*halves, early, late, bias)
+
+
+def update_kernel(bound, *refs):
+    grads, norm = refs[:5], refs[5]
+    masters, moments, squares = refs[6:12], refs[12:18], refs[18:24]
+    total, fresh = refs[24], refs[25:]
+    root = jnp.sqrt(jnp.sum(norm[...], axis=(0, 1), keepdims=True))
+    total[...] = root
+    factor = jnp.minimum(1.0, bound / root)
+    for k in range(6):
+        if k < 4:
+            grad = grads[k][...]
+        elif k == 4:
+            grad = grads[4][0, 0:8, 0 : masters[4].shape[1]]
+        else:
+            grad = grads[4][1, 0:1, 0 : masters[5].shape[1]]
+        new = adam_step(
+            masters[k][...], moments[k][...], squares[k][...], grad, factor, RATES[k]
+        )
+        for ref, item in zip((fresh[k], fresh[6 + k], fresh[12 + k]), new):
+            ref[...] = item
+
+
+def run_update(bound, grads, norm, masters, moments, squares):
+    def flat(items):
+        return [*items[:5], items[5].reshape(1, -1)]
+
+    grads = [item.reshape(-1, item.shape[-1]) for item in grads[:4]] + [grads[4]]
+    state = flat(masters) + flat(moments) + flat(squares)
+    vmem = pl.BlockSpec(memory_space=pltpu.VMEM)
+    done = pl.pallas_call(
+        functools.partial(update_kernel, bound),
+        in_specs=[vmem] * 24,
+        out_specs=[vmem] * 19,
+        out_shape=[shaped((1, 1), F32)] + [shaped(item.shape, F32) for item in state],
+        compiler_params=vmem_params(),
+        name="update_state",
+    )(*grads, norm, *state)
+    fresh = [item.reshape(-1) if k % 6 == 5 else item for k, item in enumerate(done[1:])]
+    return [done[0].reshape(()), *fresh]
+
+
+def compute(tokens, cotangent, segment_ids, valid_counts, full):
+    low_qkv, low_out, low_up, low_down, vectors, up_bias = full
     qkv, attended, lse = run_forward(segment_ids, valid_counts, tokens, vectors, low_qkv)
     (
         layer_out,
@@ -489,12 +854,12 @@
         grad_down,
         grad_up,
         grad_out_w,
-        late_vectors,
+        late,
         grad_bias,
     ) = run_feed(
         valid_counts, tokens, cotangent, attended, vectors, up_bias, low_out, low_up, low_down
     )
-    token_grad, grad_qkv_w, early_vectors = run_backward(
+    token_grad, grad_qkv_w, early = run_backward(
         segment_ids,
         valid_counts,
         tokens,
@@ -505,16 +870,38 @@
         grad_resid,
         lse,
     )
-    partial = (
-        grad_qkv_w,
-        grad_out_w,
-        grad_up,
-        grad_down,
-        early_vectors + late_vectors,
-        grad_bias.reshape(FF),
+    return layer_out, token_grad, (grad_qkv_w, grad_out_w, grad_up, grad_down), early, late, grad_bias
+
+
+def fast_body(tokens, cotangent, segment_ids, valid_counts, *state):
+    masters, moments, squares = state[:6], state[6:12], state[12:18]
+    wide = lax.axis_size("fsdp")
+    planes = wide // COLS
+    full = run_gather(planes, masters)
+    layer_out, token_grad, totals, early, late, bias = compute(
+        tokens, cotangent, segment_ids, valid_counts, full
+    )
+    *grads, norm = run_scatter(planes, D // wide, FF // wide, totals, early, late, bias)
+    bound = 0.005 * math.sqrt(tokens.shape[0] * wide * lax.axis_size("dp") * PARAMS)
+    return (layer_out, token_grad, *run_update(bound, grads, norm, masters, moments, squares))
+
+
+def plain_body(tokens, cotangent, segment_ids, valid_counts, *state):
+    masters, moments, squares = state[:6], state[6:12], state[12:18]
+    wide = lax.axis_size("fsdp")
+    replicas = lax.axis_size("dp")
+    low = [item.astype(BF16) for item in masters]
+    full = [
+        lax.all_gather(item, "fsdp", axis=1 if k == 4 else 0, tiled=True)
+        for k, item in enumerate(low)
+    ]
+    full[4] = full[4].astype(F32)
+    full[5] = full[5].astype(F32).reshape(1, FF)
+    layer_out, token_grad, totals, early, late, bias = compute(
+        tokens, cotangent, segment_ids, valid_counts, full
     )
     grads = []
-    for k, item in enumerate(partial):
+    for k, item in enumerate((*totals, early + late, bias.reshape(FF))):
         shard = lax.psum_scatter(item, "fsdp", scatter_dimension=1 if k == 4 else 0, tiled=True)
         grads.append(lax.psum(shard.astype(BF16), "dp").astype(F32))
     local_total = jnp.sum(grads[0] * grads[0])
@@ -546,8 +933,10 @@
         P(None, "fsdp"),
         P("fsdp"),
     )
+    wide, replicas = mesh.shape["fsdp"], mesh.shape["dp"]
+    fits = replicas == 2 and wide % COLS == 0 and D % (32 * wide) == 0
     return jax.shard_map(
-        body,
+        fast_body if fits else plain_body,
         mesh=mesh,
         in_specs=(rows, rows, rows, P(("fsdp", "dp")), *state, *state, *state),
         out_specs=(rows, rows, P(), *state, *state, *state),

time: 843 us -> 210 us (0.25)
  waiting for transfers between devices: 489 us -> 0 us
  blocking collectives: 209 us -> 0 us
  Pallas kernels: 93 us -> 209 us
  other arithmetic: 26.4 us -> 0 us
  between operations: 20.5 us -> 0.87 us
    reduce_scatter x4 -> x0, waiting for transfers between devices: 397 us -> none  [body(): lax.psum_scatter(item, 'fsdp', scatter_dimension=1 if k == 4 else 0, tile...]
    all_gather x3 -> x0, blocking collectives: 123 us -> none  [body(): lax.all_gather(item, 'fsdp', axis=1 if k == 4 else 0, tiled=True)]
    pallas_call x0 -> x3, Pallas kernels: none -> 116 us  [the longest x1 66 us: run_scatter(): pl.pallas_call(functools.partial(scatter_kernel, planes, per, long), in_s...]
    psum x2 -> x0, blocking collectives: 46.1 us -> none  [the longest x1 42.5 us: body(): grad_norm = jnp.sqrt(lax.psum(local_total, 'fsdp'))]
    all_gather x3 -> x0, waiting for transfers between devices: 43.9 us -> none  [body(): lax.all_gather(item, 'fsdp', axis=1 if k == 4 else 0, tiled=True)]
    unnamed x1 -> x0, blocking collectives: 39.9 us -> none
    unnamed x10 -> x0, waiting for transfers between devices: 33.4 us -> none
    psum x1 -> x0, waiting for transfers between devices: 14.8 us -> none  [body(): grads.append(lax.psum(shard.astype(BF16), 'dp').astype(F32))]
  transfers between devices with their start and end apart: 9 -> 0, of which waited for: 7 -> 0; matrix products, arithmetic and copies ran while one was open for 2% -> 0% of each run, Pallas kernels for 2% -> 0%
where the time goes in v2:
time: 210 us
  Pallas kernels  209 us (100%)
    pallas_call x1, Pallas kernels, run_scatter(): pl.pallas_call(functools.partial(scatter_kernel, planes, per, long), in_s...  66 us
    pallas_call x1, Pallas kernels, run_gather(): pl.pallas_call(functools.partial(gather_kernel, planes), in_specs=[vmem]...  46.1 us
    pallas_call x1, Pallas kernels, run_feed(): pl.pallas_call(functools.partial(feed_kernel, step, 512), grid=(rows // s...  42.1 us
    pallas_call x1, Pallas kernels, run_backward(): pl.pallas_call(functools.partial(backward_kernel, 512), grid=(rows // SEQ...  33.9 us
    pallas_call x1, Pallas kernels, run_forward(): pl.pallas_call(functools.partial(forward_kernel, 256), grid=(seqs,), in_s...  17.2 us

profile of v2, /device:TPU:0, one launch (start us, length us, event | category | flops | bytes accessed | tf_op | source)
XLA Modules:
  0.0 210.0 jit_solution(698386147661815196)
XLA Ops:
  0.7 46.1 %gather_weights.1 = (bf16[4,4,2,16,1536]{4,3,2,1,0:T(8,128)(2,1)}, bf16[4,4,2,16,512]{4,3,2,1,0:T(8,128)(2,1)}, bf16[4,4,2,16,2048]{4,3,2,1,0:T(8,128)(2,1)}, bf...) custom-call(f32[2,16,1536]{2,1,0:T(8,128)} %bitcast.33, f32[2,16,512]{2,1,0:T(8,128)} %bitcast.37, ...), custom_call_target="tpu_custom_call" | custom-call | tf_op jit(solution)/shard_map/gather_weights/pallas_call | solution.py:737
  46.7 17.2 %attend_forward.1 = (bf16[2048,1536]{1,0:T(8,128)(2,1)}, bf16[2048,512]{1,0:T(8,128)(2,1)}, f32[20,1,768]{2,1,0:T(1,128)}) custom-call(s32[2,1024]{1,0:T(2,128)} %seg.3, s32[2]{0:T(128)} %counts.5, bf16[2048,512]{1,0:T(8,128)(2,1)} %tokens.5, f32[8,512]{1,0:T(8,128)} %get-tuple-element.66.vectors, bf16[512,1536]{1,0:T(8,128)(2,1)} %bitcast.23), custom_call_target="tpu_custom_call" | custom-call | tf_op jit(solution)/shard_map/attend_forward/pallas_call | solution.py:361
  63.9 42.1 %feed_forward.1 = (bf16[2048,512]{1,0:T(8,128)(2,1)}, f32[2048,512]{1,0:T(8,128)}, bf16[2048,512]{1,0:T(8,128)(2,1)}, f32[2048,512]{1,0:T(8,128)}, f32[512,2048]...) custom-call(s32[2]{0:T(128)} %counts.5, bf16[2048,512]{1,0:T(8,128)(2,1)} %tokens.5, ...), custom_call_target="tpu_custom_call" | custom-call | tf_op jit(solution)/shard_map/feed_forward/pallas_call | solution.py:379
  106.0 33.9 %attend_backward.1 = (f32[2048,512]{1,0:T(8,128)}, f32[512,1536]{1,0:T(8,128)}, f32[8,512]{1,0:T(8,128)}) custom-call(s32[2,1024]{1,0:T(2,128)} %seg.3, s32[2]{0:T(128)} %counts.5, bf16[2048,512]{1,0:T(8,128)(2,1)} %tokens.5, f32[8,512]{1,0:T(8,128)} %get-tuple-element.66.vectors, bf16[512,1536]{1,0:T(8,128)(2,1)} %bitcast.24, ...), custom_call_target="tpu_custom_call" | custom-call | tf_op jit(solution)/shard_map/attend_backward/pallas_call | solution.py:420
  140.0 66.0 %scatter_gradients.1 = (f32[2,16,1536]{2,1,0:T(8,128)}, f32[2,16,512]{2,1,0:T(8,128)}, f32[2,16,2048]{2,1,0:T(8,128)}, f32[2,64,512]{2,1,0:T(8,128)}, f32[2,16,128]{2,1,0:T(8,128)}, /*index=5*/f32[8,128]{1,0:T(8,128)}) custom-call(f32[4,4,2,16,1536]{4,3,2,1,0:T(8,128)} %bitcast.27, f32[4,4,2,16,512]{4,3,2,1,0:T(8,128)} %bitcast.32, ...), custom_call_target="tpu_custom_call" | custom-call | tf_op jit(solution)/shard_map/scatter_gradients/pallas_call | solution.py:794
  205.9 3.9 %update_state.1 = (f32[1,1]{1,0:T(1,128)}, f32[32,1536]{1,0:T(8,128)}, f32[32,512]{1,0:T(8,128)}, f32[32,2048]{1,0:T(8,128)}, f32[128,512]{1,0:T(8,128)}, /*inde...) custom-call(f32[32,1536]{1,0:T(8,128)} %bitcast.38, ...), custom_call_target="tpu_custom_call" | custom-call | tf_op jit(solution)/shard_map/update_state/pallas_call | solution.py:835
